TPU v7x, 512 devices: a whole 4x8x8 slice. The times are simulated.
512 devices in a mesh: grp: 32 (over x, z), seq: 16 (over y, core).
Axes of the slice: x: 4, y: 8, z: 8, core: 2. Of those that a mesh axis runs over, the one named last changes fastest.
Arguments:
- query_rows: bfloat16 [512, 128, 1536], P(('grp', 'seq')), may hold values from -400 to 400
- key_rows: bfloat16 [512, 128, 1536], P(('grp', 'seq')), may hold values from -400 to 400
- value_rows: bfloat16 [512, 128, 1536], P(('grp', 'seq')), may hold values from -6 to 6
- out_grad: bfloat16 [512, 128, 1536], P(('grp', 'seq')), may hold values from -6 to 6
- proj_grad: bfloat16 [512, 3072, 128], P('grp', 'seq'), may hold values from -6 to 6
- proj_weight: bfloat16 [3072, 1536], P('seq'), may hold values from -0.15625 to 0.15625
- query_gain: float32 [1536], P('grp'), may hold values from 0.5 to 5
- key_gain: float32 [1536], P('grp'), may hold values from 0.5 to 5
- clip_of_frame: int32 [512], replicated, may hold values from 0 to 63, never falling along the last dimension, each value on 1 to 16 neighbouring positions
- patch_count: int32 [64], replicated, may hold values from 1 to 128, as said below
Outputs:
- attended: bfloat16 [512, 128, 1536], P(('grp', 'seq'))
- projected: bfloat16 [512, 3072, 128], P('grp', 'seq')
- query_grad: bfloat16 [512, 128, 1536], P(('grp', 'seq'))
- key_grad: bfloat16 [512, 128, 1536], P(('grp', 'seq'))
- value_grad: bfloat16 [512, 128, 1536], P(('grp', 'seq'))
- weight_grad: float32 [1536, 3072], P('grp', 'seq')
- query_gain_grad: float32 [1536], P('grp')
- key_gain_grad: float32 [1536], P('grp')
Inputs may be any that keep to these rules, and one draw needn't show every extreme that they name: `clip_of_frame`: the frames of a clip are consecutive; a clip has at most 16 frames, and some clip has exactly 16. `patch_count`: some clip has 128 live positions and some has 1.
All inputs are finite; a program needn't handle non-finite values.
Results may differ from a plain program's by a relative error of at most 0.039.
The roundings to bfloat16 on the way count: a program that leaves them out, or rounds other values in their place, can miss the bound.
Values may be sent and summed in bfloat16 or wider, within the bound.
A program may use at most 64 MiB of HBM per device.

v0:
```python
import jax
import jax.numpy as jnp
from jax import lax
from jax.sharding import PartitionSpec as P

HEADS = 12
HEAD_DIM = 128


EPS = 1e-06
NEGATIVE = -1e30


def extended(array, sides, width):
    for axis, dim in sides:
        count, length = (lax.axis_size(axis), array.shape[dim])
        up = [(i, (i + 1) % count) for i in range(count - 1)]
        down = [(j, i) for i, j in up]
        last = lax.slice_in_dim(array, length - width, length, axis=dim)
        initial = lax.slice_in_dim(array, 0, width, axis=dim)
        before = lax.ppermute(last, axis, up)
        after = lax.ppermute(initial, axis, down)
        array = jnp.concatenate([before, array, after], axis=dim)
    return array


def from_behind(array, axis, by):
    count = lax.axis_size(axis)
    pairs = [(i, i + by) for i in range(count) if 0 <= i + by < count]
    return lax.ppermute(array, axis, pairs)


def head_norm(features, gain_row):
    shaped = features.astype(jnp.float32).reshape(features.shape[:-1] + (HEADS, HEAD_DIM))
    inverse = lax.rsqrt(jnp.mean(shaped * shaped, axis=-1, keepdims=True) + EPS)
    normed = (shaped * inverse).reshape(features.shape) * gain_row
    return (normed.astype(jnp.bfloat16), inverse)


def norm_backward(features, gain_row, inverse, upstream):
    shaped = features.astype(jnp.float32).reshape(features.shape[:-1] + (HEADS, HEAD_DIM))
    incoming = upstream.astype(jnp.float32)
    weighted = (incoming * gain_row).reshape(shaped.shape)
    along_head = jnp.mean(weighted * shaped, axis=-1, keepdims=True)
    grad_rows = inverse * weighted - shaped * inverse * inverse * inverse * along_head
    gain_terms = incoming * (shaped * inverse).reshape(features.shape)
    gain_sum = jnp.sum(gain_terms.reshape(-1, features.shape[-1]), axis=0)
    return (grad_rows.reshape(features.shape).astype(jnp.bfloat16), gain_sum)


def split_heads(values):
    return values.reshape(values.shape[:-1] + (HEADS, HEAD_DIM))


def product(pattern, first_operand, second_operand):
    return jnp.einsum(pattern, first_operand, second_operand, preferred_element_type=jnp.float32)


def softmax_rows(scores, pair_mask, live_rows):
    masked = jnp.where(pair_mask, scores, NEGATIVE)
    row_top = jnp.max(masked, axis=-1, keepdims=True)
    spread = jnp.where(pair_mask, jnp.exp(masked - row_top), 0.0)
    row_total = jnp.where(live_rows, jnp.sum(spread, axis=-1, keepdims=True), 1.0)
    return (spread / row_total, row_top + jnp.log(row_total))


def body(
    query_rows,
    key_rows,
    value_rows,
    out_grad,
    proj_grad,
    proj_weight,
    query_gain,
    key_gain,
    clip_of_frame,
    patch_count,
):
    frames_dev, patches, channels = query_rows.shape
    seq_count = lax.axis_size("seq")
    group_count = lax.axis_size("grp")
    frames_group = frames_dev * seq_count
    patch_share = patches // seq_count
    width_share = proj_weight.shape[0]
    own_rows = frames_dev * patches
    score_scale = HEAD_DIM ** (-0.5)
    grad_flat = jnp.transpose(proj_grad, (0, 2, 1)).reshape(frames_group * patches, width_share)
    query_full, key_full = (
        lax.all_gather(query_gain, "grp", axis=0, tiled=True),
        lax.all_gather(key_gain, "grp", axis=0, tiled=True),
    )
    query_normed, query_inverse = head_norm(query_rows, query_full)
    key_normed, key_inverse = head_norm(key_rows, key_full)
    spaced = lax.all_to_all(
        jnp.stack((query_normed, key_normed, value_rows, out_grad)),
        "seq",
        split_axis=2,
        concat_axis=1,
        tiled=True,
    )
    split_rows = split_heads(spaced)
    own_query = split_rows[0]
    own_grad = split_rows[3]
    group_index = lax.axis_index("grp")
    seq_index = lax.axis_index("seq")
    border = jnp.full((frames_group,), -1, jnp.int32)
    clip_padded = jnp.concatenate([border, clip_of_frame, border])
    nearby_clip = lax.dynamic_slice_in_dim(
        clip_padded, group_index * frames_group, 3 * frames_group, 0
    )
    clip_slots = jnp.arange(patch_count.shape[0], dtype=jnp.int32)
    nearby_count = jnp.sum(
        jnp.where(nearby_clip[:, None] == clip_slots[None, :], patch_count[None, :], 0), axis=1
    )
    positions = seq_index * patch_share + jnp.arange(patch_share, dtype=jnp.int32)
    nearby_live = (positions[None, :] < nearby_count[:, None]).T
    own_clip = nearby_clip[frames_group : 2 * frames_group]
    own_live = nearby_live[:, frames_group : 2 * frames_group]
    pair_mask = ((own_clip[:, None] == nearby_clip[None, :])[None] & own_live[:, :, None])[:, None]
    live_rows = own_live[:, None, :, None]
    window = split_heads(extended(spaced[1:3], (("grp", 1),), frames_group))
    nearby_key = window[0]
    nearby_value = window[1]
    scores = product("qphe,kphe->phqk", own_query, nearby_key) * score_scale
    probabilities, log_total = softmax_rows(scores, pair_mask, live_rows)
    rounded = probabilities.astype(jnp.bfloat16)
    attended = product("phqk,kphe->qphe", rounded, nearby_value).astype(jnp.bfloat16)
    row_delta = product("qphe,qphe->phq", own_grad, attended)[..., None]
    prob_grad = product("qphe,kphe->phqk", own_grad, nearby_value)
    score_grad = (probabilities * (prob_grad - row_delta) * score_scale).astype(jnp.bfloat16)
    query_side = product("phqk,kphe->qphe", score_grad, nearby_key).astype(jnp.bfloat16)
    partial_value = jnp.stack(
        (
            product("phqk,qphe->kphe", score_grad, own_query),
            product("phqk,qphe->kphe", rounded, own_grad),
        )
    )
    from_after = from_behind(partial_value[:, :frames_group], "grp", -1)
    from_before = from_behind(partial_value[:, 2 * frames_group :], "grp", 1)
    summed = partial_value[:, frames_group : 2 * frames_group] + from_after + from_before
    key_side = summed[0].astype(jnp.bfloat16)
    value_side = summed[1].astype(jnp.bfloat16)
    outgoing = jnp.stack((attended, query_side, key_side, value_side)).reshape(
        4, frames_group, patch_share, channels
    )
    returned = lax.all_to_all(outgoing, "seq", split_axis=1, concat_axis=2, tiled=True)
    attended_time = returned[0]
    token_root = float(frames_dev * patches * group_count * seq_count) ** 0.5
    piece = lax.all_gather(attended_time.reshape(own_rows, channels), "seq", axis=0, tiled=True)
    piece_out = product("tc,dc->td", piece, proj_weight)
    out_rows = piece_out
    weight_sum = product("tc,td->cd", piece, grad_flat)
    out_rows, weight_sum = (out_rows, weight_sum)
    projected = jnp.transpose(
        out_rows.astype(jnp.bfloat16).reshape(frames_group, patches, width_share), (0, 2, 1)
    )
    weight_grad = lax.psum_scatter(weight_sum, "grp", scatter_dimension=0, tiled=True) / token_root
    query_grad, query_terms = norm_backward(query_rows, query_full, query_inverse, returned[1])
    key_grad, key_terms = norm_backward(key_rows, key_full, key_inverse, returned[2])
    gain_terms = jnp.stack((query_terms, key_terms))
    gain_total = lax.psum(
        lax.psum_scatter(gain_terms, "grp", scatter_dimension=1, tiled=True), "seq"
    )
    gain_total = gain_total / token_root
    return (
        attended_time,
        projected,
        query_grad,
        key_grad,
        returned[3],
        weight_grad,
        gain_total[0],
        gain_total[1],
    )


def solution(mesh):
    in_specs = (
        P(("grp", "seq"), None, None),
        P(("grp", "seq"), None, None),
        P(("grp", "seq"), None, None),
        P(("grp", "seq"), None, None),
        P("grp", "seq", None),
        P("seq", None),
        P("grp"),
        P("grp"),
        P(),
        P(),
    )
    out_specs = (
        P(("grp", "seq"), None, None),
        P("grp", "seq", None),
        P(("grp", "seq"), None, None),
        P(("grp", "seq"), None, None),
        P(("grp", "seq"), None, None),
        P("grp", "seq"),
        P("grp"),
        P("grp"),
    )
    return jax.shard_map(body, mesh=mesh, in_specs=in_specs, out_specs=out_specs, check_vma=False)
```

profile of v0, /device:TPU:1, one launch (start us, length us, event | category | flops | bytes accessed | tf_op | source)
XLA Modules:
  0.0 788.1 jit_solution(10526376125461244013)
XLA Ops:
  8.0 1.3 copy.143
  12.8 1.3 dynamic-slice
  15.3 122.3 %all-reduce.2 = (f32[1536]{0:T(1024)S(1)}, f32[1536]{0:T(1024)S(1)}) all-reduce(f32[1536]{0:T(1024)S(1)} %dynamic-update-slice.1, f32[1536]{0:T(1024)S(1)} %dynamic-update-slice), channel_id=1, replica_groups=mesh['grp'=32,'seq'=16] {'grp'}, use_global_device_ids=true, to_apply=%add.1 | all-reduce | flops 3072 | bytes 24576
  138.7 2.6 copy.147
  141.3 35.3 %all-to-all-start = ((bf16[4,1,128,1536]{3,0,1,2:T(4,128)(2,1)}), bf16[4,1,128,1536]{3,0,1,2:T(4,128)(2,1)S(1)}, u32[]{:S(2)}, u32[]{:S(2)}) async-start(bf16[4,1,128,1536]{3,0,1,2:T(4,128)(2,1)} %copy.147), calls=%async_computation | async-start | bytes 3145728 | tf_op jit(solution)/shard_map/all_to_all | solution.py:94
  178.0 37.0 %all-to-all-done = bf16[4,1,128,1536]{3,0,1,2:T(4,128)(2,1)S(1)} async-done(((bf16[4,1,128,1536]{3,0,1,2:T(4,128)(2,1)}), bf16[4,1,128,1536]{3,0,1,2:T(4,128)(2,1)S(1)}, u32[]{:S(2)}, u32[]{:S(2)}) %all-to-all-start) | async-done | bytes 1572896 | tf_op jit(solution)/shard_map/all_to_all | solution.py:94
  216.0 1.3 collective-permute-start
  217.3 1.5 collective-permute-start.1
  221.0 13.3 %collective-permute-done = bf16[2,16,8,1536]{3,2,1,0:T(8,128)(2,1)S(1)} collective-permute-done((bf16[2,16,8,1536]{3,2,1,0:T(8,128)(2,1)S(1)}, bf16[2,16,8,1536]{3,2,1,0:T(8,128)(2,1)S(1)}, u32[]{:S(2)}, u32[]{:S(2)}) %collective-permute-start) | collective-permute-done | bytes 786464 | tf_op jit(solution)/shard_map/ppermute | solution.py:21
  234.3 4.4 collective-permute-done.1
  240.2 3.5 fusion.41
  244.6 2.4 convolution_bitcast_fusion
  247.0 1.3 multiply_reduce_fusion
  250.2 1.3 collective-permute-start.2
  251.5 4.1 collective-permute-start.3
  257.0 30.8 %collective-permute-done.2 = f32[2,16,8,12,128]{4,1,3,2,0:T(8,128)S(1)} collective-permute-done((f32[2,16,8,12,128]{4,1,3,2,0:T(8,128)S(1)}, f32[2,16,8,12,128]{4,1,3,2,0:T(8,128)S(1)}, u32[]{:S(2)}, u32[]{:S(2)}) %collective-permute-start.2) | collective-permute-done | bytes 1572896 | tf_op jit(solution)/shard_map/ppermute | solution.py:30
  290.0 44.2 %all_to_all.8 = bf16[4,16,8,1536]{3,2,0,1:T(8,128)(2,1)S(1)} all-to-all(bf16[4,16,8,1536]{3,2,0,1:T(8,128)(2,1)S(1)} %copy.163), channel_id=1, replica_groups=mesh['grp'=32,'seq'=16] {'seq'}, dimensions={1} | all-to-all | bytes 3145728 | tf_op jit(solution)/shard_map/all_to_all | solution.py:146
  334.2 2.0 slice_bitcast_fusion.2
  336.4 1.3 reshape.489
  337.7 1.3 copy.170
  339.2 1.2 copy.167
  340.5 1.2 copy.166
  341.6 2.5 copy.169
  344.1 1.6 multiply_reduce_fusion.3
  347.1 1.2 copy.182
  348.4 28.1 %all-gather.2.cloned.1.call-done = bf16[2048,1536]{1,0:T(8,128)(2,1)} async-done(((bf16[128,1536]{1,0:T(8,128)(2,1)}), bf16[2048,1536]{1,0:T(8,128)(2,1)}) %all-gather.2.cloned.1.call-update) | async-done | bytes 6291472 | tf_op jit(solution)/shard_map/all_gather | solution.py:149
  376.5 5.8 fusion.25
  384.2 170.4 %reduce-scatter.7.cloned.1.call-done = f32[48,2]{1,0:T(8,128)} async-done(((f32[1536,2]{1,0:T(8,128)}), f32[48,2]{1,0:T(8,128)}) %reduce-scatter.7.cloned.1.call-update) | async-done | bytes 400
  555.5 28.9 %psum.7 = f32[2,48]{1,0:T(2,128)S(1)} all-reduce(f32[2,48]{1,0:T(2,128)S(1)} %copy.183), channel_id=1, replica_groups=mesh['grp'=32,'seq'=16] {'seq'}, use_global_device_ids=true, to_apply=%region_11.12 | all-reduce | flops 96 | bytes 768 | tf_op jit(solution)/shard_map/psum | solution.py:161
  584.9 5.0 fusion.9
  591.0 188.3 %reduce-scatter.5.cloned.1.call-done = f32[48,192]{1,0:T(8,128)} async-done(((f32[1536,192]{1,0:T(8,128)}), f32[48,192]{1,0:T(8,128)}) %reduce-scatter.5.cloned.1.call-update) | async-done | bytes 36880 | tf_op jit(solution)/shard_map/reduce_scatter | solution.py:157
  779.3 1.4 broadcast_multiply_fusion
  (113 shorter events, 23.5 us)
Async XLA Ops:
  8.0 368.5 %copy-start = (bf16[16,192,128]{2,1,0:T(8,128)(2,1)S(1)}, bf16[16,192,128]{2,1,0:T(8,128)(2,1)}, u32[]{:S(2)}) copy-start(bf16[16,192,128]{2,1,0:T(8,128)(2,1)} %param.14) | copy-start | bytes 2359300
  8.0 2.4 copy-start.11
  9.3 2.3 copy-start.12
  10.4 1.5 copy-start.13
  10.4 127.2 %copy-start.14 = (f32[128,12]{0,1:T(8,128)}, f32[128,12]{0,1:T(8,128)S(1)}, u32[]{:S(2)}) copy-start(f32[128,12]{0,1:T(8,128)S(1)} %add_rsqrt_fusion.1) | copy-start | bytes 18436
  10.6 4.1 copy-start.21
  10.6 4.4 copy-start.22
  11.6 126.5 %copy-start.16 = (f32[128,12]{0,1:T(8,128)}, f32[128,12]{0,1:T(8,128)S(1)}, u32[]{:S(2)}) copy-start(f32[128,12]{0,1:T(8,128)S(1)} %add_rsqrt_fusion) | copy-start | bytes 18436
  137.5 1.0 copy-start.7
  141.3 35.4 %copy-start.19 = (s32[512]{0:T(512)S(1)}, s32[512]{0:T(512)}, u32[]{:S(2)}) copy-start(s32[512]{0:T(512)} %param.18) | copy-start | bytes 6148
  141.3 35.6 %copy-start.23 = (s32[64]{0:T(128)S(1)}, s32[64]{0:T(128)}, u32[]{:S(2)}) copy-start(s32[64]{0:T(128)} %param.19) | copy-start | bytes 772
  141.3 73.7 %all-to-all-start = ((bf16[4,1,128,1536]{3,0,1,2:T(4,128)(2,1)}), bf16[4,1,128,1536]{3,0,1,2:T(4,128)(2,1)S(1)}, u32[]{:S(2)}, u32[]{:S(2)}) async-start(bf16[4,1,128,1536]{3,0,1,2:T(4,128)(2,1)} %copy.147), calls=%async_computation | async-start | bytes 3145728 | tf_op jit(solution)/shard_map/all_to_all | solution.py:94
  176.6 199.9 %all-gather.2.cloned.1.call-start = ((), (), s32[]{:S(2)}) async-start(), calls=%async_computation.4 | async-start | bytes 6684672 | tf_op jit(solution)/shard_map/all_gather | solution.py:149
  177.2 38.7 %copy-start.18 = (pred[8,16]{1,0:T(8,128)(4,1)}, pred[8,16]{1,0:T(8,128)(4,1)S(1)}, u32[]{:S(2)}) copy-start(pred[8,16]{1,0:T(8,128)(4,1)S(1)} %slice.73) | copy-start | bytes 388
  216.0 18.3 %collective-permute-start = (bf16[2,16,8,1536]{3,2,1,0:T(8,128)(2,1)S(1)}, bf16[2,16,8,1536]{3,2,1,0:T(8,128)(2,1)S(1)}, u32[]{:S(2)}, u32[]{:S(2)}) collective-permute-start(bf16[2,16,8,1536]{3,2,1,0:T(8,128)(2,1)S(1)} %bitcast.153), channel_id=1, source_target_pairs={{0,16},{16,32},{32,48},{48,64},{64,80},{80,96},{96,112},{112,128},... | collective-permute-start | bytes 2359304 | tf_op jit(solution)/shard_map/ppermute | solution.py:21
  217.3 21.4 %collective-permute-start.1 = (bf16[2,16,8,1536]{3,2,1,0:T(8,128)(2,1)S(1)}, bf16[2,16,8,1536]{3,2,1,0:T(8,128)(2,1)S(1)}, u32[]{:S(2)}, u32[]{:S(2)}) collective-permute-start(bf16[2,16,8,1536]{3,2,1,0:T(8,128)(2,1)S(1)} %bitcast.154), channel_id=1, source_target_pairs={{16,0},{32,16},{48,32},{64,48},{80,64},{96,80},{112,96},{128,112},... | collective-permute-start | bytes 2359304 | tf_op jit(solution)/shard_map/ppermute | solution.py:22
  244.6 2.4 copy-start.8
  244.6 2.4 copy-start.9
  244.6 2.4 copy-start.10
  250.2 37.5 %collective-permute-start.2 = (f32[2,16,8,12,128]{4,1,3,2,0:T(8,128)S(1)}, f32[2,16,8,12,128]{4,1,3,2,0:T(8,128)S(1)}, u32[]{:S(2)}, u32[]{:S(2)}) collective-permute-start(f32[2,16,8,12,128]{4,1,3,2,0:T(8,128)S(1)} %get-tuple-element.54), channel_id=1, source_target_pairs={{16,0},{32,16},{48,32},{64,48},{80,64},{96,80},{112,96},{128,112},... | collective-permute-start | bytes 4718600 | tf_op jit(solution)/shard_map/ppermute | solution.py:30
  251.5 37.0 %collective-permute-start.3 = (f32[2,16,8,12,128]{4,1,3,2,0:T(8,128)S(1)}, f32[2,16,8,12,128]{4,1,3,2,0:T(8,128)S(1)}, u32[]{:S(2)}, u32[]{:S(2)}) collective-permute-start(f32[2,16,8,12,128]{4,1,3,2,0:T(8,128)S(1)} %get-tuple-element.55), channel_id=1, source_target_pairs={{0,16},{16,32},{32,48},{48,64},{64,80},{80,96},{96,112},{112,128},... | collective-permute-start | bytes 4718600 | tf_op jit(solution)/shard_map/ppermute | solution.py:30
  336.2 218.5 %reduce-scatter.7.cloned.1.call-start = ((), (), s32[]{:S(2)}) async-start(), calls=%async_computation.6 | async-start | bytes 811008
  339.2 1.3 copy-start.6
  340.5 3.7 copy-start.1
  341.6 4.1 copy-start.2
  344.1 1.6 copy-start.3
  344.1 1.9 copy-start.4
  344.1 1.9 copy-start.5
  344.1 1.9 copy-start.15
  344.1 1.9 copy-start.17
  348.3 430.9 %reduce-scatter.5.cloned.1.call-start = ((), (), s32[]{:S(2)}) async-start(), calls=%async_computation.5 | async-start | bytes 1622016 | tf_op jit(solution)/shard_map/reduce_scatter | solution.py:157
  382.4 202.5 %copy-start.20 = (bf16[192,1536]{1,0:T(8,128)(2,1)S(1)}, bf16[192,1536]{1,0:T(8,128)(2,1)}, u32[]{:S(2)}) copy-start(bf16[192,1536]{1,0:T(8,128)(2,1)} %param.15) | copy-start | bytes 1769476
Sparse Core Ops, SparseCore 0:
  336.3 40.2 all-gather.1
Sparse Core Ops, SparseCore 1:
  348.4 206.2 reduce-scatter.6
  559.0 220.3 reduce-scatter.4
where the time goes:
time: 793 us; the launch traced here: 788 us
  waiting for transfers between devices  473 us (60%)
  blocking collectives  195 us (25%)
  starting transfers between devices  43.8 us (6%)
  local copies, waits for them, and re-layouts  25.5 us (3%)
  matrix products  20.4 us (3%)
  between operations  16.7 us (2%)
  other arithmetic  13.1 us (2%)
    reduce_scatter x1, waiting for transfers between devices, body(): lax.psum_scatter(weight_sum, 'grp', scatter_dimension=0, tiled=True)  188 us
    unnamed x4, waiting for transfers between devices  170 us
    unnamed x1, blocking collectives  122 us
    all_to_all x1, blocking collectives, body(): lax.all_to_all(outgoing, 'seq', split_axis=1, concat_axis=2, tiled=True)  44.2 us
    all_to_all x1, waiting for transfers between devices, body(): lax.all_to_all(jnp.stack((query_normed, key_normed, value_rows, out_grad)...  37 us
    all_to_all x1, starting transfers between devices, body(): lax.all_to_all(jnp.stack((query_normed, key_normed, value_rows, out_grad)...  35.3 us
    ppermute x2, waiting for transfers between devices, from_behind(): return lax.ppermute(array, axis, pairs)  31.6 us
    psum x1, blocking collectives, body(): lax.psum(lax.psum_scatter(gain_terms, 'grp', scatter_dimension=1, tiled=T...  28.9 us
  transfers between devices with their start and end apart: 8, of which 8 were waited for; matrix products, arithmetic and copies ran while one was open for 4% of the time, Pallas kernels for 0%

commit v1 on v0

v1 whole, which is shorter than its diff:
```python
import functools

import jax
import jax.numpy as jnp
from jax import lax
from jax.experimental import pallas as pl
from jax.experimental.pallas import tpu as pltpu
from jax.sharding import PartitionSpec as P

HEADS = 12
HEAD_DIM = 128
EPS = 1e-06
NEGATIVE = -1e30
SCALE = HEAD_DIM ** (-0.5)
MESH = pl.DeviceIdType.MESH

POS = 16
CORES = 2
CHUNKS = 2
CHUNK_HEADS = HEADS // (CORES * CHUNKS)
CH = CHUNK_HEADS * HEAD_DIM
HALF = CHUNKS * CH
X = CORES * CHUNKS
BLOCK_POS = 4
LANES = 256
VMEM_LIMIT = 60 * 1024 * 1024


def dot(a, b, dims):
    return lax.dot_general(a, b, (dims, ((), ())), preferred_element_type=jnp.float32)


def place():
    seq_count = lax.axis_size("seq")
    group_count = lax.axis_size("grp")
    grp, seq = lax.axis_index("grp"), lax.axis_index("seq")
    z_count, y_count = group_count // X, seq_count // CORES
    return (
        grp, seq, z_count, y_count,
        lax.div(grp, z_count), lax.rem(grp, z_count),
        lax.div(seq, CORES), lax.rem(seq, CORES),
    )


def wait_bytes(ref, sem):
    pltpu.make_async_copy(ref, ref, sem).wait()


def remote(src, dst, send_sem, recv_sem, device):
    return pltpu.make_async_remote_copy(
        src_ref=src, dst_ref=dst, send_sem=send_sem, recv_sem=recv_sem, device_id=device, device_id_type=MESH
    )


def loop(low, high, step):
    def one(i, carry):
        step(i)
        return carry

    lax.fori_loop(low, high, one, 0)


def greet(with_neighbours):
    grp, seq, z_count, y_count, x, z, y, core = place()
    seq_count, group_count = y_count * CORES, z_count * X
    barrier = pltpu.get_barrier_semaphore()

    def signal(device):
        pl.semaphore_signal(barrier, inc=1, device_id=device, device_id_type=MESH)

    loop(1, seq_count, lambda d: signal({"seq": lax.rem(seq + d, seq_count)}))
    if z_count > 1:
        loop(1, z_count, lambda d: signal({"grp": x * z_count + lax.rem(z + d, z_count)}))
    loop(1, X, lambda d: signal({"grp": lax.rem(x + d, X) * z_count + z}))
    total = seq_count - 1 + z_count - 1 + X - 1
    if with_neighbours:
        signal({"grp": lax.rem(grp + 1, group_count)})
        signal({"grp": lax.rem(grp + group_count - 1, group_count)})
        total += 2
    pl.semaphore_wait(barrier, total)


def exchange_kernel(
    q, k, v, g, gain, win, full, stage, gz, gx, gs, load_sem, send_sem, recv_sem, halo_send, halo_recv, gain_send, gain_recv
):
    grp, seq, z_count, y_count, x, z, y, core = place()
    seq_count, group_count = y_count * CORES, z_count * X
    loads = [pltpu.make_async_copy(ref, stage.at[i], load_sem.at[i]) for i, ref in enumerate((q, k, v, g))]
    for load in loads:
        load.start()
    greet(True)
    if z_count > 1:
        loop(
            1, z_count,
            lambda d: remote(
                gain, gz.at[z], gain_send.at[0], gain_recv.at[0], {"grp": x * z_count + lax.rem(z + d, z_count)}
            ).start(),
        )
    for load in loads:
        load.wait()
    for c in range(CHUNKS):
        def send(i, c=c):
            odd = lax.rem(i, 2)
            dy = odd * lax.div(i + 1, 2) + (1 - odd) * (y_count - lax.div(i, 2))
            other = lax.rem(y + dy, y_count)
            for cc in range(CORES):
                remote(
                    stage.at[:, other, :, pl.ds(cc * HALF + c * CH, CH)], win.at[c, 0, :, seq],
                    send_sem.at[c], recv_sem.at[c], {"seq": other * CORES + cc},
                ).start()

        pltpu.make_async_copy(
            stage.at[:, y, :, pl.ds(pl.multiple_of(core * HALF + c * CH, HEAD_DIM), CH)],
            win.at[c, 0, :, seq], recv_sem.at[c],
        ).start()
        remote(
            stage.at[:, y, :, pl.ds(pl.multiple_of((1 - core) * HALF + c * CH, HEAD_DIM), CH)],
            win.at[c, 0, :, seq], send_sem.at[c], recv_sem.at[c], {"seq": y * CORES + 1 - core},
        ).start()
        loop(1, y_count, send)
    gz[z] = gain[...]
    if z_count > 1:
        wait_bytes(gz.at[pl.ds(0, z_count - 1)], gain_recv.at[0])
    gs[...] = jnp.sum(gz[...], axis=0)
    loop(
        1, X,
        lambda d: remote(
            gs, gx.at[x], gain_send.at[1], gain_recv.at[1], {"grp": lax.rem(x + d, X) * z_count + z}
        ).start(),
    )
    gx[x] = gs[...]
    wait_bytes(gx.at[pl.ds(0, X - 1)], gain_recv.at[1])
    full[...] = jnp.sum(gx[...], axis=0)
    halos = []
    for c in range(CHUNKS):
        wait_bytes(win.at[c, 0], recv_sem.at[c])
        for way, step in enumerate((1, group_count - 1)):
            halo = remote(
                win.at[c, 0], win.at[c, 1 + way], halo_send.at[c, way], halo_recv.at[c, way],
                {"grp": lax.rem(grp + step, group_count)},
            )
            halo.start()
            halos.append(halo)
    for halo in halos:
        halo.wait()
    for c in range(CHUNKS):
        wait_bytes(win.at[c, 0, :, pl.ds(0, seq_count - 1)], send_sem.at[c])
    if z_count > 1:
        wait_bytes(gz.at[pl.ds(0, z_count - 1)], gain_send.at[0])
    wait_bytes(gx.at[pl.ds(0, X - 1)], gain_send.at[1])


def mean_lanes(values):
    return jnp.mean(values, axis=-1, keepdims=True)


def attend(win, gain, code_col, code_row, limit, perm, unperm, base, ret, att, normed, held, bias, back):
    frames = win.shape[2]
    rows = frames * POS
    wide = BLOCK_POS * frames
    bias[...] = jnp.where(code_col[...] == code_row[...], 0.0, NEGATIVE)

    def gather(slot):
        for a in range(4):
            moved = dot(perm[...], win[slot, a].reshape(rows, CH), ((1,), (0,)))
            for h in range(CHUNK_HEADS):
                part = moved[:, h * HEAD_DIM : (h + 1) * HEAD_DIM]
                if a < 2:
                    inverse = lax.rsqrt(mean_lanes(part * part) + EPS)
                    part_normed = part * inverse * gain[a : a + 1, h * HEAD_DIM : (h + 1) * HEAD_DIM]
                    normed[a, h, slot] = part_normed.astype(jnp.bfloat16)

                    @pl.when(slot == 0)
                    def _():
                        held[a, h] = part
                else:
                    normed[a, h, slot] = part.astype(jnp.bfloat16)

    loop(0, 3, gather)
    totals = []
    for h in range(CHUNK_HEADS):
        lanes = slice(h * HEAD_DIM, (h + 1) * HEAD_DIM)

        def block(b, sums, h=h, lanes=lanes):
            at = pl.ds(pl.multiple_of(b * wide, wide), wide)
            query, key, value, grad = (normed[a, h, :, at, :].reshape(3 * wide, HEAD_DIM) for a in range(4))
            scores = dot(query, key, ((1,), (1,))) * SCALE + bias[...]
            prob_grad = dot(grad, value, ((1,), (1,)))
            spread = jnp.exp(scores - jnp.max(scores, axis=-1, keepdims=True))
            live = jnp.where(limit[...] > base + b * BLOCK_POS, 1.0, 0.0)
            probs = spread * (live / jnp.sum(spread, axis=-1, keepdims=True))
            rounded = probs.astype(jnp.bfloat16)
            attended = dot(rounded, value, ((1,), (0,))).astype(jnp.bfloat16)
            delta = jnp.sum(grad.astype(jnp.float32) * attended.astype(jnp.float32), axis=-1, keepdims=True)
            score_grad = (probs * (prob_grad - delta) * SCALE).astype(jnp.bfloat16)
            back[0, at, lanes] = attended[:wide]
            back[3, at, lanes] = dot(rounded[:, :wide], grad, ((0,), (0,))).astype(jnp.bfloat16)
            ups = (
                dot(score_grad[:wide], key, ((1,), (0,))),
                dot(score_grad[:, :wide], query, ((0,), (0,))),
            )
            new = []
            for a in range(2):
                up = ups[a].astype(jnp.bfloat16).astype(jnp.float32)
                rows_in = held[a, h, at, :]
                inverse = lax.rsqrt(mean_lanes(rows_in * rows_in) + EPS)
                weighted = up * gain[a : a + 1, lanes]
                along = mean_lanes(weighted * rows_in)
                scaled = rows_in * inverse
                back[1 + a, at, lanes] = (inverse * weighted - scaled * inverse * inverse * along).astype(jnp.bfloat16)
                new.append(sums[a] + jnp.sum(up * scaled, axis=0, keepdims=True))
            return tuple(new)

        zero = jnp.zeros((1, HEAD_DIM), jnp.float32)
        totals.append(lax.fori_loop(0, POS // BLOCK_POS, block, (zero, zero)))
    for a in range(4):
        out = dot(unperm[...], back[a], ((1,), (0,))).astype(jnp.bfloat16).reshape(frames, POS, CH)
        if a == 0:
            att[pl.ds(0, frames)] = out
        else:
            ret[a - 1] = out
    row = lax.broadcasted_iota(jnp.int32, (POS, CH), 0)
    packed = jnp.zeros((POS, CH), jnp.float32)
    for a in range(2):
        total = jnp.concatenate([sums[a] for sums in totals], axis=1)
        packed = packed + hi_lo(total, row, 2 * a)
    att[frames] = packed.astype(jnp.bfloat16)


def hi_lo(total, row, first):
    high = total.astype(jnp.bfloat16).astype(jnp.float32)
    low = total - high
    return jnp.where(row == first, high, 0.0) + jnp.where(row == first + 1, low, 0.0)


def attend_kernel(win, gain, code_col, code_row, limit, perm, unperm, ret, att, normed, held, bias, back):
    base = lax.div(lax.axis_index("seq"), CORES) * POS
    attend(
        win.at[0], gain, code_col, code_row, limit, perm, unperm, base, ret.at[0], att.at[0], normed, held, bias, back
    )


def collect_kernel(
    ret, att, grad, weight, rows_out, att_out, proj_out, wide_out, ag, acc, turn, zsend, zrecv, xsend, xrecv,
    ret_send, ret_recv, own_sem, ring_send, ring_recv, sib_send, sib_recv, z_send, z_recv, x_send, x_recv, att_sem,
):
    grp, seq, z_count, y_count, x, z, y, core = place()
    seq_count = y_count * CORES
    frames, width, patches = grad.shape
    far = y_count // 2
    share = CH // z_count
    half = (frames + 1) // 2
    halves = ((0, half), (half, frames + 1 - half))
    greet(False)
    neighbours = (lax.rem(y + 1, y_count) * CORES + core, lax.rem(y + y_count - 1, y_count) * CORES + core)
    sibling = y * CORES + 1 - core

    def ring_copy(c, way, hop, ref=None):
        at = lax.rem(y + hop * (y_count - 1 if way == 0 else 1), y_count)
        src, dst = ag.at[c, core, at], ag.at[c, core, at]
        if ref is not None:
            src = ref
        if hop + 1 == far:
            src, dst = src.at[pl.ds(*halves[way])], dst.at[pl.ds(*halves[way])]
        return remote(src, dst, ring_send.at[c, way, hop], ring_recv.at[c, way, hop], {"seq": neighbours[way]})

    def ring_wait(c, way, hop):
        at = lax.rem(y + (hop + 1) * (y_count - 1 if way == 0 else 1), y_count)
        ref = ag.at[c, core, at]
        if hop + 1 == far:
            ref = ref.at[pl.ds(*halves[way])]
        wait_bytes(ref, ring_recv.at[c, way, hop])
        return ref

    def to_sibling(c, src, dst):
        remote(src, dst, sib_send.at[c], sib_recv.at[c], {"seq": sibling}).start()

    for c in range(CHUNKS):
        for way in range(2):
            ring_copy(c, way, 0, att.at[c]).start()
        to_sibling(c, att.at[c], ag.at[c, core, y])
        pltpu.make_async_copy(att.at[c], ag.at[c, core, y], own_sem.at[c]).start()
    for c in range(CHUNKS):
        lanes = pl.ds(pl.multiple_of(core * HALF + c * CH, HEAD_DIM), CH)
        mine = rows_out.at[:, y, :, lanes]

        def send(d, c=c, mine=mine):
            other = lax.rem(seq + d, seq_count)
            remote(ret.at[c, :, other], mine, ret_send.at[c], ret_recv, {"seq": other}).start()

        pltpu.make_async_copy(ret.at[c, :, seq], mine, ret_recv).start()
        loop(1, seq_count, send)

    def weigh(c):
        for kc in range(CORES):
            def pair(i):
                left = jnp.concatenate([grad[2 * i], grad[2 * i + 1]], axis=1)
                right = jnp.concatenate([ag[c, kc, :, 2 * i + j].reshape(patches, CH) for j in range(2)], axis=0)
                turn[pl.ds(0, width)] += dot(left, right, ((1,), (0,)))

            turn[...] = jnp.zeros_like(turn)
            loop(0, frames // 2, pair)
            terms = jnp.sum(ag[c, kc, :, frames].astype(jnp.float32), axis=0)
            row = lax.broadcasted_iota(jnp.int32, (POS, CH), 0)
            packed = hi_lo(terms[0:1] + terms[1:2], row, 0) + hi_lo(terms[2:3] + terms[3:4], row, 2)
            turn[pl.ds(width, POS)] = packed
            zsend[c, :, kc] = turn[...].T.astype(jnp.bfloat16).reshape(z_count, share, LANES)
        if z_count > 1:
            def give(d):
                other = lax.rem(z + d, z_count)
                remote(
                    zsend.at[c, other], zrecv.at[c, z], z_send.at[c], z_recv.at[c], {"grp": x * z_count + other}
                ).start()

            loop(1, z_count, give)
        zrecv[c, z] = zsend[c, z]

    def project(c):
        def frame(f):
            total = jnp.zeros((width, patches), jnp.float32)
            for kc in range(CORES):
                lanes = slice(kc * HALF + c * CH, kc * HALF + (c + 1) * CH)
                total = total + dot(weight[:, lanes], ag[c, kc, :, f].reshape(patches, CH), ((1,), (1,)))
            if c > 0:
                total = total + acc[f]
            if c + 1 < CHUNKS:
                acc[f] = total
            else:
                proj_out[f] = total.astype(jnp.bfloat16)

        loop(0, frames, frame)

    for c in range(CHUNKS):
        for hop in range(far):
            for way in range(2):
                ref = ring_wait(c, way, hop)
                if hop + 1 < far:
                    ring_copy(c, way, hop + 1).start()
                to_sibling(c, ref, ref)
        wait_bytes(ag.at[c, core, y], own_sem.at[c])
        wait_bytes(ag.at[c, 1 - core], sib_recv.at[c])
        for kc in range(CORES):
            lanes = pl.ds(kc * HALF + c * CH, CH)
            pltpu.make_async_copy(ag.at[c, kc, :, seq], att_out.at[:, :, lanes], att_sem).start()
        weigh(c)
        project(c)
    for c in range(CHUNKS):
        if z_count > 1:
            wait_bytes(zrecv.at[c, pl.ds(0, z_count - 1)], z_recv.at[c])
        sums = jnp.sum(zrecv[c].astype(jnp.float32), axis=0)
        for kc in range(CORES):
            xsend[kc * CHUNKS + c] = sums[kc]

    def last(d):
        other = lax.rem(x + d, X)
        remote(xsend.at[other], xrecv.at[x], x_send, x_recv, {"grp": other * z_count + z}).start()

    loop(1, X, last)
    xrecv[x] = xsend[x]
    wait_bytes(att_out, att_sem)
    wait_bytes(rows_out, ret_recv)
    wait_bytes(xrecv.at[pl.ds(0, X - 1)], x_recv)
    token_root = float(frames * patches * z_count * X) ** 0.5
    wide_out[...] = jnp.sum(xrecv[...], axis=0) / token_root
    wait_bytes(xsend.at[pl.ds(0, X - 1)], x_send)
    for c in range(CHUNKS):
        if z_count > 1:
            wait_bytes(zsend.at[c, pl.ds(0, z_count - 1)], z_send.at[c])
        wait_bytes(ret.at[c, :, pl.ds(0, seq_count - 1)], ret_send.at[c])
        wait_bytes(ag.at[c, core], sib_send.at[c])
        for way in range(2):
            for hop in range(far):
                ring_copy(c, way, hop).wait_send()


def body(
    query_rows,
    key_rows,
    value_rows,
    out_grad,
    proj_grad,
    proj_weight,
    query_gain,
    key_gain,
    clip_of_frame,
    patch_count,
):
    bf16, f32 = jnp.bfloat16, jnp.float32
    patches, channels = query_rows.shape[1:]
    seq_count, group_count = lax.axis_size("seq"), lax.axis_size("grp")
    y_count, z_count = seq_count // CORES, group_count // X
    frames = seq_count
    width = proj_weight.shape[0]
    share = channels // group_count
    rows = frames * POS
    wide = BLOCK_POS * frames
    group_index, seq_index = lax.axis_index("grp"), lax.axis_index("seq")
    vmem, anywhere = pl.BlockSpec(memory_space=pltpu.VMEM), pl.BlockSpec(memory_space=pl.ANY)
    dma = pltpu.SemaphoreType.DMA

    placed = jnp.zeros((8, channels), f32)
    placed = lax.dynamic_update_slice(placed, jnp.stack((query_gain, key_gain)), (0, group_index * share))
    placed = lax.dynamic_slice_in_dim(placed, lax.rem(seq_index, CORES) * HALF, HALF, 1)

    win, gains = pl.pallas_call(
        exchange_kernel,
        out_shape=(
            jax.ShapeDtypeStruct((CHUNKS, 3, 4, frames, POS, CH), bf16),
            jax.ShapeDtypeStruct((8, HALF), f32),
        ),
        in_specs=[anywhere] * 4 + [vmem],
        out_specs=(anywhere, vmem),
        scratch_shapes=[
            pltpu.VMEM((4, y_count, POS, channels), bf16),
            pltpu.VMEM((z_count, 8, HALF), f32),
            pltpu.VMEM((X, 8, HALF), f32),
            pltpu.VMEM((8, HALF), f32),
            dma((4,)),
            dma((CHUNKS,)),
            dma((CHUNKS,)),
            dma((CHUNKS, 2)),
            dma((CHUNKS, 2)),
            dma((2,)),
            dma((2,)),
        ],
        compiler_params=pltpu.CompilerParams(collective_id=0, has_side_effects=True, vmem_limit_bytes=VMEM_LIMIT),
        name="exchange",
    )(*(a.reshape(y_count, POS, channels) for a in (query_rows, key_rows, value_rows, out_grad)), placed)

    border = jnp.full((frames,), -1, jnp.int32)
    clip_padded = jnp.concatenate([border, clip_of_frame, border])
    nearby = lax.dynamic_slice_in_dim(clip_padded, group_index * frames, 3 * frames, 0).reshape(3, frames)
    nearby = jnp.stack((nearby[1], nearby[0], nearby[2]))
    slots = jnp.arange(patch_count.shape[0], dtype=jnp.int32)
    counts = jnp.sum(jnp.where(nearby[..., None] == slots, patch_count, 0), axis=-1)
    offset = jnp.arange(BLOCK_POS, dtype=jnp.int32)[None, :, None]
    codes = (nearby[:, None, :] * BLOCK_POS + offset).reshape(3 * wide)
    limit = (counts[:, None, :] - offset).reshape(3 * wide, 1)
    index = jnp.arange(rows, dtype=jnp.int32)
    source = index % frames * POS + index // frames
    perm = (source[:, None] == index[None, :]).astype(bf16)

    whole = lambda shape: pl.BlockSpec(shape, lambda c: (0,) * len(shape))
    ret, att = pl.pallas_call(
        attend_kernel,
        grid=(CHUNKS,),
        out_shape=(
            jax.ShapeDtypeStruct((CHUNKS, 3, frames, POS, CH), bf16),
            jax.ShapeDtypeStruct((CHUNKS, frames + 1, POS, CH), bf16),
        ),
        in_specs=[
            pl.BlockSpec((1, 3, 4, frames, POS, CH), lambda c: (c, 0, 0, 0, 0, 0)),
            pl.BlockSpec((8, CH), lambda c: (0, c)),
            whole((3 * wide, 1)),
            whole((1, 3 * wide)),
            whole((3 * wide, 1)),
            whole((rows, rows)),
            whole((rows, rows)),
        ],
        out_specs=(
            pl.BlockSpec((1, 3, frames, POS, CH), lambda c: (c, 0, 0, 0, 0)),
            pl.BlockSpec((1, frames + 1, POS, CH), lambda c: (c, 0, 0, 0)),
        ),
        scratch_shapes=[
            pltpu.VMEM((4, CHUNK_HEADS, 3, rows, HEAD_DIM), bf16),
            pltpu.VMEM((2, CHUNK_HEADS, rows, HEAD_DIM), f32),
            pltpu.VMEM((3 * wide, 3 * wide), f32),
            pltpu.VMEM((4, rows, CH), bf16),
        ],
        compiler_params=pltpu.CompilerParams(vmem_limit_bytes=VMEM_LIMIT),
        name="attend",
    )(win, gains, codes[:, None], codes[None, :], limit, perm, perm.T)

    far = y_count // 2
    rows_out, att_out, projected, wide_out = pl.pallas_call(
        collect_kernel,
        out_shape=(
            jax.ShapeDtypeStruct((3, y_count, POS, channels), bf16),
            jax.ShapeDtypeStruct((y_count, POS, channels), bf16),
            jax.ShapeDtypeStruct((frames, width, patches), bf16),
            jax.ShapeDtypeStruct((share, LANES), f32),
        ),
        in_specs=[anywhere, anywhere, vmem, vmem],
        out_specs=(anywhere, anywhere, vmem, vmem),
        scratch_shapes=[
            pltpu.VMEM((CHUNKS, CORES, y_count, frames + 1, POS, CH), bf16),
            pltpu.VMEM((frames, width, patches), f32),
            pltpu.VMEM((LANES, CH), f32),
            pltpu.VMEM((CHUNKS, z_count, CORES, share, LANES), bf16),
            pltpu.VMEM((CHUNKS, z_count, CORES, share, LANES), bf16),
            pltpu.VMEM((X, share, LANES), f32),
            pltpu.VMEM((X, share, LANES), f32),
            dma((CHUNKS,)),
            dma,
            dma((CHUNKS,)),
            dma((CHUNKS, 2, far)),
            dma((CHUNKS, 2, far)),
            dma((CHUNKS,)),
            dma((CHUNKS,)),
            dma((CHUNKS,)),
            dma((CHUNKS,)),
            dma,
            dma,
            dma,
        ],
        compiler_params=pltpu.CompilerParams(collective_id=1, has_side_effects=True, vmem_limit_bytes=VMEM_LIMIT),
        name="collect",
    )(ret, att, proj_grad, proj_weight)

    shape = (1, patches, channels)
    return (
        att_out.reshape(shape),
        projected,
        rows_out[0].reshape(shape),
        rows_out[1].reshape(shape),
        rows_out[2].reshape(shape),
        wide_out[:, :width],
        wide_out[:, width] + wide_out[:, width + 1],
        wide_out[:, width + 2] + wide_out[:, width + 3],
    )


def solution(mesh):
    rows = P(("grp", "seq"), None, None)
    in_specs = (rows, rows, rows, rows, P("grp", "seq", None), P("seq", None), P("grp"), P("grp"), P(), P())
    out_specs = (rows, P("grp", "seq", None), rows, rows, rows, P("grp", "seq"), P("grp"), P("grp"))
    return jax.shard_map(body, mesh=mesh, in_specs=in_specs, out_specs=out_specs, check_vma=False)
```

time: 793 us -> 227 us (0.29)
  waiting for transfers between devices: 473 us -> 0 us
  Pallas kernels: 0 us -> 213 us
  blocking collectives: 195 us -> 0 us
  starting transfers between devices: 43.8 us -> 0 us
  matrix products: 20.4 us -> 0 us
  local copies, waits for them, and re-layouts: 25.5 us -> 7.81 us
  between operations: 16.7 us -> 0.7 us
  other arithmetic: 13.1 us -> 4.76 us
    pallas_call x0 -> x3, Pallas kernels: none -> 213 us  [the longest x1 105 us: body(): pl.pallas_call(collect_kernel, out_shape=(jax.ShapeDtypeStruct((3, y_coun...]
    reduce_scatter x1 -> x0, waiting for transfers between devices: 188 us -> none  [body(): lax.psum_scatter(weight_sum, 'grp', scatter_dimension=0, tiled=True)]
    unnamed x4 -> x0, waiting for transfers between devices: 170 us -> none
    unnamed x1 -> x0, blocking collectives: 122 us -> none
    ppermute x4 -> x0, waiting for transfers between devices: 49.3 us -> none  [the longest x2 31.6 us: from_behind(): return lax.ppermute(array, axis, pairs)]
    all_to_all x1 -> x0, blocking collectives: 44.2 us -> none  [body(): lax.all_to_all(outgoing, 'seq', split_axis=1, concat_axis=2, tiled=True)]
    all_to_all x1 -> x0, waiting for transfers between devices: 37 us -> none  [body(): lax.all_to_all(jnp.stack((query_normed, key_normed, value_rows, out_grad)...]
    all_to_all x1 -> x0, starting transfers between devices: 35.3 us -> none  [body(): lax.all_to_all(jnp.stack((query_normed, key_normed, value_rows, out_grad)...]
  transfers between devices with their start and end apart: 8 -> 0, of which waited for: 8 -> 0; matrix products, arithmetic and copies ran while one was open for 4% -> 0% of each run, Pallas kernels for 0% -> 0%
where the time goes in v1:
time: 227 us; the launch traced here: 226 us
  Pallas kernels  213 us (94%)
  local copies, waits for them, and re-layouts  7.81 us (3%)
  other arithmetic  4.76 us (2%)
    pallas_call x1, Pallas kernels, body(): pl.pallas_call(collect_kernel, out_shape=(jax.ShapeDtypeStruct((3, y_coun...  105 us
    pallas_call x1, Pallas kernels, body(): pl.pallas_call(exchange_kernel, out_shape=(jax.ShapeDtypeStruct((CHUNKS,...  73.2 us
    pallas_call x1, Pallas kernels, body(): pl.pallas_call(attend_kernel, grid=(CHUNKS,), out_shape=(jax.ShapeDtypeSt...  35.1 us

profile of v1, /device:TPU:1, one launch (start us, length us, event | category | flops | bytes accessed | tf_op | source)
XLA Modules:
  0.0 226.4 jit_solution(9718961967698379990)
XLA Ops:
  0.6 0.7 pad_maximum_fusion
  1.3 0.8 pad_add_fusion
  2.1 0.1 dynamic_slice.7
  2.2 0.1 slice_bitcast_fusion.2
  2.3 0.9 select_reduce_fusion
  3.2 0.7 add.89.code_row
  3.8 0.3 dynamic_update_slice.3
  4.1 0.6 constant_dynamic-slice_fusion.gain
  4.7 0.7 add.97.code_col
  5.5 0.7 sub.33.limit
  6.2 0.8 fusion.1
  7.0 73.2 %exchange.1 = (bf16[2,3,4,16,16,384]{5,4,3,2,1,0:T(8,128)(2,1)}, f32[8,768]{1,0:T(8,128)}) custom-call(bf16[8,16,1536]{2,1,0:T(8,128)(2,1)} %bitcast.22, bf16[8,16,1536]{2,1,0:T(8,128)(2,1)} %bitcast.23, bf16[8,16,1536]{2,1,0:T(8,128)(2,1)} %bitcast.24, bf16[8,16,1536]{2,1,0:T(8,128)(2,1)} %bitcast.25, f32[8,768]{1,0:T(8,128)} %constant_dynamic-slice_fusion.gain), custom_call_target="tpu_custom_call" | custom-call | tf_op jit(solution)/shard_map/exchange/pallas_call | solution.py:405
  80.1 35.1 %attend.1 = (bf16[2,3,16,16,384]{4,3,2,1,0:T(8,128)(2,1)}, bf16[2,17,16,384]{3,2,1,0:T(8,128)(2,1)}) custom-call(bf16[2,3,4,16,16,384]{5,4,3,2,1,0:T(8,128)(2,1)} %get-tuple-element.16.win, f32[8,768]{1,0:T(8,128)} %get-tuple-element.17.gain, s32[192,1]{1,0:T(8,128)} %add.97.code_col, s32[1,192]{1,0:T(1,128)} %add.89.code_row, s32[192,1]{1,0:T(8,128)} %sub.33.limit, ...), custom_call_target="tpu_custom_call" | custom-call | tf_op jit(solution)/shard_map/attend/pallas_call | solution.py:444
  115.3 104.9 %collect.1 = (bf16[3,8,16,1536]{3,2,1,0:T(8,128)(2,1)}, bf16[8,16,1536]{2,1,0:T(8,128)(2,1)}, bf16[16,192,128]{2,1,0:T(8,128)(2,1)}, f32[48,256]{1,0:T(8,128)}) custom-call(bf16[2,3,16,16,384]{4,3,2,1,0:T(8,128)(2,1)} %get-tuple-element.18.ret, bf16[2,17,16,384]{3,2,1,0:T(8,128)(2,1)} %get-tuple-element.19.att, bf16[16,192,128]{2,1,0:T(8,128)(2,1)} %grad.1, ...), custom_call_target="tpu_custom_call" | custom-call | tf_op jit(solution)/shard_map/collect/pallas_call | solution.py:475
  220.1 1.7 add_reduce_fusion
  221.8 0.0 copy-start.2
  221.8 0.0 copy-start
  221.8 2.4 %fusion.6 = (bf16[1,8,16,1536]{3,2,1,0:T(8,128)(2,1)}, bf16[1,8,16,1536]{3,2,1,0:T(8,128)(2,1)}, bf16[1,8,16,1536]{3,2,1,0:T(8,128)(2,1)}) fusion(bf16[3,8,16,1536]{3,2,1,0:T(8,128)(2,1)} %get-tuple-element.22), kind=kLoop, calls=%fused_computation.27 | loop fusion | bytes 2359296 | tf_op jit(solution)/shard_map/slice | solution.py:516
  224.2 0.0 copy-done.2
  224.2 0.0 copy-start.1
  224.2 0.7 copy.26
  224.9 0.0 copy-done
  224.9 0.9 copy.27
  225.8 0.0 copy-done.1
  225.8 0.6 copy.28
  (6 shorter events, 0.0 us)
Async XLA Ops:
  221.8 2.4 %copy-start.2 = (bf16[8,16,1536]{2,1,0:T(8,128)(2,1)S(1)}, bf16[8,16,1536]{2,1,0:T(8,128)(2,1)}, u32[]{:S(2)}) copy-start(bf16[8,16,1536]{2,1,0:T(8,128)(2,1)} %get-tuple-element.20) | copy-start | bytes 1179652
  221.8 3.1 %copy-start = (bf16[16,192,128]{2,1,0:T(8,128)(2,1)S(1)}, bf16[16,192,128]{2,1,0:T(8,128)(2,1)}, u32[]{:S(2)}) copy-start(bf16[16,192,128]{2,1,0:T(8,128)(2,1)} %get-tuple-element.45) | copy-start | bytes 2359300
  224.2 1.6 copy-start.1

commit v2 on v1

v2 whole, which is shorter than its diff:
```python
import jax
import jax.numpy as jnp
from jax import lax
from jax.experimental import pallas as pl
from jax.experimental.pallas import tpu as pltpu
from jax.sharding import PartitionSpec as P

HEADS = 12
HEAD_DIM = 128
EPS = 1e-06
NEGATIVE = -1e30
SCALE = HEAD_DIM ** (-0.5)
MESH = pl.DeviceIdType.MESH

POS = 16
CORES = 2
CHUNKS = 3
CHUNK_HEADS = HEADS // (CORES * CHUNKS)
CH = CHUNK_HEADS * HEAD_DIM
HALF = CHUNKS * CH
X = 4
BLOCK_POS = 8
LANES = 256
VMEM_LIMIT = 60 * 1024 * 1024


def dot(a, b, dims):
    return lax.dot_general(a, b, (dims, ((), ())), preferred_element_type=jnp.float32)


def place():
    seq_count = lax.axis_size("seq")
    group_count = lax.axis_size("grp")
    grp, seq = lax.axis_index("grp"), lax.axis_index("seq")
    z_count, y_count = group_count // X, seq_count // CORES
    return (
        grp, seq, z_count, y_count,
        lax.div(grp, z_count), lax.rem(grp, z_count),
        lax.div(seq, CORES), lax.rem(seq, CORES),
    )


def wait_bytes(ref, sem):
    pltpu.make_async_copy(ref, ref, sem).wait()


def remote(src, dst, send_sem, recv_sem, device):
    return pltpu.make_async_remote_copy(
        src_ref=src, dst_ref=dst, send_sem=send_sem, recv_sem=recv_sem, device_id=device, device_id_type=MESH
    )


def loop(low, high, step):
    def one(i, carry):
        step(i)
        return carry

    lax.fori_loop(low, high, one, 0)


def greet():
    grp, seq, z_count, y_count, x, z, y, core = place()
    seq_count, group_count = y_count * CORES, z_count * X
    barrier = pltpu.get_barrier_semaphore()

    def signal(device):
        pl.semaphore_signal(barrier, inc=1, device_id=device, device_id_type=MESH)

    loop(1, seq_count, lambda d: signal({"seq": lax.rem(seq + d, seq_count)}))
    if z_count > 1:
        loop(1, z_count, lambda d: signal({"grp": x * z_count + lax.rem(z + d, z_count)}))
    loop(1, X, lambda d: signal({"grp": lax.rem(x + d, X) * z_count + z}))
    for step in (1, group_count - 1):
        signal({"grp": lax.rem(grp + step, group_count)})
    pl.semaphore_wait(barrier, seq_count + z_count + X - 1)


def mean_lanes(values):
    return jnp.mean(values, axis=-1, keepdims=True)


def hi_lo(total, row, first):
    high = total.astype(jnp.bfloat16).astype(jnp.float32)
    low = total - high
    return jnp.where(row == first, high, 0.0) + jnp.where(row == first + 1, low, 0.0)


def iota(shape, dim):
    return lax.broadcasted_iota(jnp.int32, shape, dim)


def fused_kernel(
    q, k, v, g, query_gain, key_gain, clip, count, grad, weight,
    rows_out, proj_out, wide_out, gain_out,
    stage, win, normed, held, bias, limit, perms, back, ret, att, ag, tokens, w, turn, zall, zrecv, xsend, xrecv, gz, gx, gs, gains,
    load_sem, send_sem, recv_sem, halo_send, halo_recv, gain_send, gain_recv,
    ret_send, ret_recv, own_sem, ring_send, ring_recv, sib_send, sib_recv, z_send, z_recv, x_send, x_recv,
):
    grp, seq, z_count, y_count, x, z, y, core = place()
    seq_count, group_count = y_count * CORES, z_count * X
    frames, width, patches = grad.shape
    rows = frames * POS
    wide = BLOCK_POS * frames
    share = HALF * CORES // group_count
    far = y_count // 2
    f32, bf16 = jnp.float32, jnp.bfloat16

    loads = [pltpu.make_async_copy(ref, stage.at[i], load_sem.at[i]) for i, ref in enumerate((q, k, v, g))]
    for load in loads:
        load.start()
    for f in range(frames):
        pltpu.make_async_copy(grad.at[f], tokens.at[:, pl.ds(f * patches, patches)], load_sem.at[4]).start()
    pltpu.make_async_copy(weight, w, load_sem.at[5]).start()

    lane, sub = iota((8, HALF), 1), iota((8, HALF), 0)
    gs[...] = jnp.zeros_like(gs)

    def put_gain(i):
        at = lane == grp * share + i - core * HALF
        gs[...] += jnp.where(at & (sub == 0), query_gain[i], 0.0) + jnp.where(at & (sub == 1), key_gain[i], 0.0)

    loop(0, share, put_gain)
    greet()

    if z_count > 1:
        loop(
            1, z_count,
            lambda d: remote(
                gs, gz.at[z], gain_send.at[0], gain_recv.at[0], {"grp": x * z_count + lax.rem(z + d, z_count)}
            ).start(),
        )
    for load in loads:
        load.wait()
    for c in range(CHUNKS):
        def spread_out(i, c=c):
            odd = lax.rem(i, 2)
            dy = odd * lax.div(i + 1, 2) + (1 - odd) * (y_count - lax.div(i, 2))
            other = lax.rem(y + dy, y_count)
            for cc in range(CORES):
                remote(
                    stage.at[:, other, :, pl.ds(cc * HALF + c * CH, CH)], win.at[c, 0, :, seq],
                    send_sem.at[c], recv_sem.at[c], {"seq": other * CORES + cc},
                ).start()

        loop(1, y_count, spread_out)
        remote(
            stage.at[:, y, :, pl.ds(pl.multiple_of((1 - core) * HALF + c * CH, HEAD_DIM), CH)],
            win.at[c, 0, :, seq], send_sem.at[c], recv_sem.at[c], {"seq": y * CORES + 1 - core},
        ).start()
        pltpu.make_async_copy(
            stage.at[:, y, :, pl.ds(pl.multiple_of(core * HALF + c * CH, HEAD_DIM), CH)],
            win.at[c, 0, :, seq], recv_sem.at[c],
        ).start()

    def code_of(index, slot):
        at = (grp + (0, -1, 1)[slot]) * frames + index
        inside = (at >= 0) & (at < frames * group_count)
        own_clip = clip[lax.rem(at + frames * group_count, frames * group_count)]
        return jnp.where(inside, own_clip, -1), jnp.where(inside, count[own_clip], 0)

    col, row = iota((3 * wide, 1), 0), iota((1, 3 * wide), 1)
    col_code, row_code = jnp.zeros((3 * wide, 1), jnp.int32), jnp.zeros((1, 3 * wide), jnp.int32)
    col_count = jnp.zeros((3 * wide, 1), jnp.int32)
    for slot in range(3):
        def put_code(i, carry, slot=slot):
            col_code, row_code, col_count = carry
            code, most = code_of(i, slot)

            def here(index):
                return (lax.div(index, wide) == slot) & (lax.rem(index, frames) == i)

            return (
                jnp.where(here(col), code, col_code),
                jnp.where(here(row), code, row_code),
                jnp.where(here(col), most, col_count),
            )

        col_code, row_code, col_count = lax.fori_loop(0, frames, put_code, (col_code, row_code, col_count))

    def position(index):
        return lax.div(lax.rem(index, wide), frames)

    bias[...] = jnp.where((col_code == row_code) & (position(col) == position(row)), 0.0, NEGATIVE)
    limit[...] = col_count - position(col)
    down, across = iota((rows, rows), 0), iota((rows, rows), 1)
    for i, (one, other) in enumerate(((down, across), (across, down))):
        source = lax.rem(one, frames) * POS + lax.div(one, frames)
        perms[i] = jnp.where(source == other, 1.0, 0.0).astype(bf16)

    gz[z] = gs[...]
    if z_count > 1:
        wait_bytes(gz.at[pl.ds(0, z_count - 1)], gain_recv.at[0])
        wait_bytes(gz.at[pl.ds(0, z_count - 1)], gain_send.at[0])
    gs[...] = jnp.sum(gz[...], axis=0)
    loop(
        1, X,
        lambda d: remote(
            gs, gx.at[x], gain_send.at[1], gain_recv.at[1], {"grp": lax.rem(x + d, X) * z_count + z}
        ).start(),
    )
    gx[x] = gs[...]

    def halo(c, way):
        return remote(
            win.at[c, 0], win.at[c, 1 + way], halo_send.at[c, way], halo_recv.at[c, way],
            {"grp": lax.rem(grp + (1, group_count - 1)[way], group_count)},
        )

    def to_neighbours(c):
        wait_bytes(win.at[c, 0], recv_sem.at[c])
        for way in range(2):
            halo(c, way).start()

    def attend(c, between):
        lanes_of = [slice(h * HEAD_DIM, (h + 1) * HEAD_DIM) for h in range(CHUNK_HEADS)]
        gain_of = [
            [gains[a : a + 1, c * CH + h * HEAD_DIM : c * CH + (h + 1) * HEAD_DIM] for a in range(2)]
            for h in range(CHUNK_HEADS)
        ]

        def gather(slot):
            for a in range(4):
                moved = dot(perms[0], win[c, slot, a].reshape(rows, CH), ((1,), (0,)))
                for h in range(CHUNK_HEADS):
                    part = moved[:, lanes_of[h]]
                    if a < 2:
                        inverse = lax.rsqrt(mean_lanes(part * part) + EPS)
                        normed[a, h, slot] = (part * inverse * gain_of[h][a]).astype(bf16)

                        @pl.when(slot == 0)
                        def _():
                            held[a, h] = part
                    else:
                        normed[a, h, slot] = part.astype(bf16)

        loop(0, 3, gather)
        between[0]()

        def block(b, sums):
            at = pl.ds(pl.multiple_of(b * wide, wide), wide)
            live = jnp.where(limit[...] > y * POS + b * BLOCK_POS, 1.0, 0.0)
            new = []
            for h in range(CHUNK_HEADS):
                query, key, value, cotangent = (
                    normed[a, h, :, at, :].reshape(3 * wide, HEAD_DIM) for a in range(4)
                )
                scores = dot(query, key, ((1,), (1,))) * SCALE + bias[...]
                prob_grad = dot(cotangent, value, ((1,), (1,)))
                spread = jnp.exp(scores - jnp.max(scores, axis=-1, keepdims=True))
                probs = spread * (live / jnp.sum(spread, axis=-1, keepdims=True))
                rounded = probs.astype(bf16)
                attended = dot(rounded, value, ((1,), (0,))).astype(bf16)
                delta = jnp.sum(cotangent.astype(f32) * attended.astype(f32), axis=-1, keepdims=True)
                score_grad = (probs * (prob_grad - delta) * SCALE).astype(bf16)
                back[0, at, lanes_of[h]] = attended[:wide]
                back[3, at, lanes_of[h]] = dot(rounded[:, :wide], cotangent, ((0,), (0,))).astype(bf16)
                ups = (
                    dot(score_grad[:wide], key, ((1,), (0,))),
                    dot(score_grad[:, :wide], query, ((0,), (0,))),
                )
                for a in range(2):
                    up = ups[a].astype(bf16).astype(f32)
                    rows_in = held[a, h, at, :]
                    inverse = lax.rsqrt(mean_lanes(rows_in * rows_in) + EPS)
                    weighted = up * gain_of[h][a]
                    along = mean_lanes(weighted * rows_in)
                    scaled = rows_in * inverse
                    back[1 + a, at, lanes_of[h]] = (
                        inverse * weighted - scaled * inverse * inverse * along
                    ).astype(bf16)
                    new.append(sums[len(new)] + jnp.sum(up * scaled, axis=0, keepdims=True))
            return tuple(new)

        zero = jnp.zeros((1, HEAD_DIM), f32)
        sums = lax.fori_loop(0, POS // BLOCK_POS, block, (zero,) * (2 * CHUNK_HEADS))
        between[1]()
        for a in range(4):
            out = dot(perms[1], back[a], ((1,), (0,))).astype(bf16).reshape(frames, POS, CH)
            if a == 0:
                att[c, pl.ds(0, frames)] = out
            else:
                ret[c, a - 1] = out
        at_row = iota((POS, CH), 0)
        packed = jnp.zeros((POS, CH), f32)
        for a in range(2):
            packed = packed + hi_lo(jnp.concatenate(sums[a::2], axis=1), at_row, 2 * a)
        att[c, frames] = packed.astype(bf16)

    neighbours = (lax.rem(y + 1, y_count) * CORES + core, lax.rem(y + y_count - 1, y_count) * CORES + core)
    sibling = y * CORES + 1 - core
    first_part = (frames + 1) // 2
    halves = ((0, first_part), (first_part, frames + 1 - first_part))

    def ring_copy(c, way, hop, ref=None):
        at = lax.rem(y + hop * (y_count - 1 if way == 0 else 1), y_count)
        src, dst = ag.at[c, core, at], ag.at[c, core, at]
        if ref is not None:
            src = ref
        if hop + 1 == far:
            src, dst = src.at[pl.ds(*halves[way])], dst.at[pl.ds(*halves[way])]
        return remote(src, dst, ring_send.at[c, way, hop], ring_recv.at[c, way, hop], {"seq": neighbours[way]})

    def to_sibling(c, src, dst):
        remote(src, dst, sib_send.at[c], sib_recv.at[c], {"seq": sibling}).start()

    def ring_step(c, hop):
        for way in range(2):
            at = lax.rem(y + (hop + 1) * (y_count - 1 if way == 0 else 1), y_count)
            ref = ag.at[c, core, at]
            if hop + 1 == far:
                ref = ref.at[pl.ds(*halves[way])]
            wait_bytes(ref, ring_recv.at[c, way, hop])
            if hop + 1 < far:
                ring_copy(c, way, hop + 1).start()
            to_sibling(c, ref, ref)

    def give_back(c):
        for way in range(2):
            ring_copy(c, way, 0, att.at[c]).start()
        to_sibling(c, att.at[c], ag.at[c, core, y])
        pltpu.make_async_copy(att.at[c], ag.at[c, core, y], own_sem.at[c]).start()
        mine = rows_out.at[pl.ds(0, 3), y, :, pl.ds(pl.multiple_of(core * HALF + c * CH, HEAD_DIM), CH)]

        def send(d):
            other = lax.rem(seq + d, seq_count)
            remote(ret.at[c, :, other], mine, ret_send.at[c], ret_recv, {"seq": other}).start()

        pltpu.make_async_copy(ret.at[c, :, seq], mine, ret_recv).start()
        loop(1, seq_count, send)

    units = 2 * z_count
    turn[...] = jnp.zeros_like(turn)

    def weigh(c):
        wait_bytes(ag.at[c, core, y], own_sem.at[c])
        wait_bytes(ag.at[c, 1 - core], sib_recv.at[c])
        for kc in range(CORES):
            pltpu.make_async_copy(
                ag.at[c, kc, :, seq], rows_out.at[3, :, :, pl.ds(kc * HALF + c * CH, CH)], ret_recv
            ).start()
            right = jnp.concatenate([ag[c, kc, :, f].reshape(patches, CH) for f in range(frames)], axis=0)
            turn[pl.ds(0, width)] = dot(tokens[...], right, ((1,), (0,)))
            terms = jnp.sum(ag[c, kc, :, frames].astype(f32), axis=0)
            at_row = iota((POS, CH), 0)
            packed = hi_lo(terms[0:1] + terms[1:2], at_row, 0) + hi_lo(terms[2:3] + terms[3:4], at_row, 2)
            turn[pl.ds(width, POS)] = packed
            zall[kc, pl.ds(c * CH, CH)] = turn[...].T.astype(bf16)
        if z_count > 1:
            for unit in range(units * c // CHUNKS, units * (c + 1) // CHUNKS):
                pair, owner = unit // z_count, unit % z_count

                @pl.when(z != owner)
                def _(unit=unit, pair=pair, owner=owner):
                    remote(
                        zall.at[:, pl.ds(unit * share, share)], zrecv.at[pair, z], z_send.at[pair], z_recv.at[pair],
                        {"grp": x * z_count + owner},
                    ).start()

    def project():
        def frame_pair(i):
            left = jnp.concatenate(
                [
                    jnp.concatenate(
                        [ag[c, kc, :, 2 * i + j].reshape(patches, CH) for kc in range(CORES) for c in range(CHUNKS)], axis=1
                    )
                    for j in range(2)
                ],
                axis=0,
            )
            total = dot(w[...], left, ((1,), (1,))).astype(bf16)
            for j in range(2):
                proj_out[2 * i + j] = total[:, j * patches : (j + 1) * patches]

        loop(0, frames // 2, frame_pair)

    def steps(*which):
        def run():
            for c, hop in which:
                if hop < far:
                    ring_step(c, hop)

        return run

    to_neighbours(0)
    wait_bytes(gx.at[pl.ds(0, X - 1)], gain_recv.at[1])
    gains[...] = jnp.sum(gx[...], axis=0)
    to_neighbours(1)
    for way in range(2):
        halo(0, way).wait_recv()
    attend(0, (steps(), steps()))
    give_back(0)
    to_neighbours(2)
    for way in range(2):
        halo(1, way).wait_recv()
    attend(1, (steps((0, 0)), steps((0, 1))))
    give_back(1)
    for way in range(2):
        halo(2, way).wait_recv()
    attend(2, (steps((0, 2), (1, 0)), steps((0, 3), (1, 1))))
    give_back(2)
    for load in (pltpu.make_async_copy(tokens, tokens, load_sem.at[4]), pltpu.make_async_copy(weight, w, load_sem.at[5])):
        load.wait()
    steps((1, 2), (2, 0))()
    weigh(0)
    steps((1, 3), (2, 1))()
    weigh(1)
    steps((2, 2), (2, 3))()
    weigh(2)
    project()
    for pair in range(2):
        if z_count > 1:
            wait_bytes(zrecv.at[pair, pl.ds(0, z_count - 1)], z_recv.at[pair])
        own = zall[:, pl.ds(pl.multiple_of((pair * z_count + z) * share, POS), share)]
        zrecv[pair, z] = own
        sums = jnp.sum(zrecv[pair].astype(f32), axis=0)
        for kc in range(CORES):
            xsend[2 * kc + pair] = sums[kc]

    def last(d):
        other = lax.rem(x + d, X)
        remote(xsend.at[other], xrecv.at[x], x_send, x_recv, {"grp": other * z_count + z}).start()

    loop(1, X, last)
    xrecv[x] = xsend[x]
    for c in range(CHUNKS):
        wait_bytes(win.at[c, 0, :, pl.ds(0, seq_count - 1)], send_sem.at[c])
        wait_bytes(ret.at[c, :, pl.ds(0, seq_count - 1)], ret_send.at[c])
        wait_bytes(ag.at[c, core], sib_send.at[c])
        for way in range(2):
            halo(c, way).wait_send()
            for hop in range(far):
                ring_copy(c, way, hop).wait_send()
    if z_count > 1:
        for pair in range(2):
            wait_bytes(zrecv.at[pair, pl.ds(0, z_count - 1)], z_send.at[pair])
    wait_bytes(gx.at[pl.ds(0, X - 1)], gain_send.at[1])
    wait_bytes(rows_out, ret_recv)
    wait_bytes(xrecv.at[pl.ds(0, X - 1)], x_recv)
    token_root = float(frames * patches * group_count) ** 0.5
    total = jnp.sum(xrecv[...], axis=0) / token_root
    wide_out[...] = total[:, :width]
    terms = total.T
    gain_out[0:1] = terms[width : width + 1] + terms[width + 1 : width + 2]
    gain_out[1:2] = terms[width + 2 : width + 3] + terms[width + 3 : width + 4]
    wait_bytes(xsend.at[pl.ds(0, X - 1)], x_send)


def body(
    query_rows,
    key_rows,
    value_rows,
    out_grad,
    proj_grad,
    proj_weight,
    query_gain,
    key_gain,
    clip_of_frame,
    patch_count,
):
    bf16, f32 = jnp.bfloat16, jnp.float32
    patches, channels = query_rows.shape[1:]
    seq_count, group_count = lax.axis_size("seq"), lax.axis_size("grp")
    y_count, z_count = seq_count // CORES, group_count // X
    frames = seq_count
    width = proj_weight.shape[0]
    share = channels // group_count
    rows = frames * POS
    wide = BLOCK_POS * frames
    far = y_count // 2
    vmem, smem = pl.BlockSpec(memory_space=pltpu.VMEM), pl.BlockSpec(memory_space=pltpu.SMEM)
    anywhere = pl.BlockSpec(memory_space=pl.ANY)
    dma = pltpu.SemaphoreType.DMA
    rows_out, projected, wide_out, gain_out = pl.pallas_call(
        fused_kernel,
        out_shape=(
            jax.ShapeDtypeStruct((4, y_count, POS, channels), bf16),
            jax.ShapeDtypeStruct((frames, width, patches), bf16),
            jax.ShapeDtypeStruct((share, width), f32),
            jax.ShapeDtypeStruct((2, share), f32),
        ),
        in_specs=[anywhere] * 4 + [smem] * 4 + [anywhere] * 2,
        out_specs=(anywhere, vmem, vmem, vmem),
        scratch_shapes=[
            pltpu.VMEM((4, y_count, POS, channels), bf16),
            pltpu.VMEM((CHUNKS, 3, 4, frames, POS, CH), bf16),
            pltpu.VMEM((4, CHUNK_HEADS, 3, rows, HEAD_DIM), bf16),
            pltpu.VMEM((2, CHUNK_HEADS, rows, HEAD_DIM), f32),
            pltpu.VMEM((3 * wide, 3 * wide), f32),
            pltpu.VMEM((3 * wide, 1), jnp.int32),
            pltpu.VMEM((2, rows, rows), bf16),
            pltpu.VMEM((4, rows, CH), bf16),
            pltpu.VMEM((CHUNKS, 3, frames, POS, CH), bf16),
            pltpu.VMEM((CHUNKS, frames + 1, POS, CH), bf16),
            pltpu.VMEM((CHUNKS, CORES, y_count, frames + 1, POS, CH), bf16),
            pltpu.VMEM((width, frames * patches), bf16),
            pltpu.VMEM((width, channels), bf16),
            pltpu.VMEM((LANES, CH), f32),
            pltpu.VMEM((CORES, HALF, LANES), bf16),
            pltpu.VMEM((2, z_count, CORES, share, LANES), bf16),
            pltpu.VMEM((X, share, LANES), f32),
            pltpu.VMEM((X, share, LANES), f32),
            pltpu.VMEM((z_count, 8, HALF), f32),
            pltpu.VMEM((X, 8, HALF), f32),
            pltpu.VMEM((8, HALF), f32),
            pltpu.VMEM((8, HALF), f32),
            dma((6,)),
            dma((CHUNKS,)),
            dma((CHUNKS,)),
            dma((CHUNKS, 2)),
            dma((CHUNKS, 2)),
            dma((2,)),
            dma((2,)),
            dma((CHUNKS,)),
            dma,
            dma((CHUNKS,)),
            dma((CHUNKS, 2, far)),
            dma((CHUNKS, 2, far)),
            dma((CHUNKS,)),
            dma((CHUNKS,)),
            dma((2,)),
            dma((2,)),
            dma,
            dma,
        ],
        compiler_params=pltpu.CompilerParams(collective_id=0, has_side_effects=True, vmem_limit_bytes=VMEM_LIMIT),
        name="fused",
    )(
        *(a.reshape(y_count, POS, channels) for a in (query_rows, key_rows, value_rows, out_grad)),
        query_gain, key_gain, clip_of_frame, patch_count, proj_grad, proj_weight,
    )
    shape = (1, patches, channels)
    return (
        rows_out[3].reshape(shape),
        projected,
        rows_out[0].reshape(shape),
        rows_out[1].reshape(shape),
        rows_out[2].reshape(shape),
        wide_out,
        gain_out[0],
        gain_out[1],
    )


def solution(mesh):
    rows = P(("grp", "seq"), None, None)
    in_specs = (rows, rows, rows, rows, P("grp", "seq", None), P("seq", None), P("grp"), P("grp"), P(), P())
    out_specs = (rows, P("grp", "seq", None), rows, rows, rows, P("grp", "seq"), P("grp"), P("grp"))
    return jax.shard_map(body, mesh=mesh, in_specs=in_specs, out_specs=out_specs, check_vma=False)
```

time: 227 us -> 137 us (0.60)
  Pallas kernels: 213 us -> 132 us
  other arithmetic: 4.76 us -> 0 us
  local copies, waits for them, and re-layouts: 7.81 us -> 4.62 us
    pallas_call x3 -> x1, Pallas kernels: 213 us -> 132 us  [body(): pl.pallas_call(fused_kernel, out_shape=(jax.ShapeDtypeStruct((4, y_count,...]
where the time goes in v2:
time: 137 us
  Pallas kernels  132 us (96%)
  local copies, waits for them, and re-layouts  4.62 us (3%)
    pallas_call x1, Pallas kernels, body(): pl.pallas_call(fused_kernel, out_shape=(jax.ShapeDtypeStruct((4, y_count,...  132 us

profile of v2, /device:TPU:1, one launch (start us, length us, event | category | flops | bytes accessed | tf_op | source)
XLA Modules:
  0.0 137.3 jit_solution(16891230969460776601)
XLA Ops:
  0.6 132.0 %fused.1 = (bf16[4,8,16,1536]{3,2,1,0:T(8,128)(2,1)}, bf16[16,192,128]{2,1,0:T(8,128)(2,1)}, f32[48,192]{1,0:T(8,128)}, f32[2,48]{1,0:T(2,128)}) custom-call(bf16[8,16,1536]{2,1,0:T(8,128)(2,1)} %bitcast.16, bf16[8,16,1536]{2,1,0:T(8,128)(2,1)} %bitcast.17, bf16[8,16,1536]{2,1,0:T(8,128)(2,1)} %bitcast.18, bf16[8,16,1536]{2,1,0:T(8,128)(2,1)} %bitcast.19, ...), custom_call_target="tpu_custom_call" | custom-call | tf_op jit(solution)/shard_map/fused/pallas_call | solution.py:473
  132.7 0.0 copy-start.2
  132.7 0.0 copy-start
  132.7 2.6 %fusion = (bf16[1,8,16,1536]{3,2,1,0:T(8,128)(2,1)}, bf16[1,8,16,1536]{3,2,1,0:T(8,128)(2,1)}, bf16[1,8,16,1536]{3,2,1,0:T(8,128)(2,1)}, bf16[1,8,16,1536]{3,2,1,0:T(8,128)(2,1)}) fusion(bf16[4,8,16,1536]{3,2,1,0:T(8,128)(2,1)} %get-tuple-element.12), kind=kLoop, calls=%fused_computation.2 | loop fusion | bytes 3145728 | tf_op jit(solution)/shard_map/slice | solution.py:537
  135.3 0.0 copy-start.1
  135.3 0.0 copy-done.2
  135.3 0.5 slice_bitcast_fusion
  135.8 0.0 copy-done
  135.8 0.9 copy.20
  136.7 0.0 copy-done.1
  136.7 0.6 copy.21
Async XLA Ops:
  132.7 2.6 %copy-start.2 = (f32[2,48]{1,0:T(2,128)S(1)}, f32[2,48]{1,0:T(2,128)}, u32[]{:S(2)}) copy-start(f32[2,48]{1,0:T(2,128)} %get-tuple-element.15) | copy-start | bytes 1156
  132.7 3.1 %copy-start = (bf16[16,192,128]{2,1,0:T(8,128)(2,1)S(1)}, bf16[16,192,128]{2,1,0:T(8,128)(2,1)}, u32[]{:S(2)}) copy-start(bf16[16,192,128]{2,1,0:T(8,128)(2,1)} %get-tuple-element.31) | copy-start | bytes 2359300
  135.3 1.4 %copy-start.1 = (f32[48,192]{1,0:T(8,128)S(1)}, f32[48,192]{1,0:T(8,128)}, u32[]{:S(2)}) copy-start(f32[48,192]{1,0:T(8,128)} %get-tuple-element.35) | copy-start | bytes 110596

commit v3 on v2

--- a/solution.py
+++ b/solution.py
@@ -21,7 +21,7 @@
 X = 4
 BLOCK_POS = 8
 LANES = 256
-VMEM_LIMIT = 60 * 1024 * 1024
+VMEM_LIMIT = 28 * 1024 * 1024
 
 
 def dot(a, b, dims):
@@ -67,12 +67,8 @@
         pl.semaphore_signal(barrier, inc=1, device_id=device, device_id_type=MESH)
 
     loop(1, seq_count, lambda d: signal({"seq": lax.rem(seq + d, seq_count)}))
-    if z_count > 1:
-        loop(1, z_count, lambda d: signal({"grp": x * z_count + lax.rem(z + d, z_count)}))
-    loop(1, X, lambda d: signal({"grp": lax.rem(x + d, X) * z_count + z}))
-    for step in (1, group_count - 1):
-        signal({"grp": lax.rem(grp + step, group_count)})
-    pl.semaphore_wait(barrier, seq_count + z_count + X - 1)
+    loop(1, group_count, lambda d: signal({"grp": lax.rem(grp + d, group_count)}))
+    return lambda: pl.semaphore_wait(barrier, seq_count + group_count - 2)
 
 
 def mean_lanes(values):
@@ -90,11 +86,12 @@
 
 
 def fused_kernel(
-    q, k, v, g, query_gain, key_gain, clip, count, grad, weight,
+    q, k, v, g, query_gain_in, key_gain_in, clip_in, count_in, grad, weight,
     rows_out, proj_out, wide_out, gain_out,
-    stage, win, normed, held, bias, limit, perms, back, ret, att, ag, tokens, w, turn, zall, zrecv, xsend, xrecv, gz, gx, gs, gains,
+    stage, win, normed, held, bias, limit, perms, back, ret, att, ag, tokens, w, turn, zall, shares, gz, gx, gs, gains,
+    query_gain, key_gain, clip, count,
     load_sem, send_sem, recv_sem, halo_send, halo_recv, gain_send, gain_recv,
-    ret_send, ret_recv, own_sem, ring_send, ring_recv, sib_send, sib_recv, z_send, z_recv, x_send, x_recv,
+    ret_send, ret_recv, own_sem, ring_send, ring_recv, sib_send, sib_recv, share_send, share_recv,
 ):
     grp, seq, z_count, y_count, x, z, y, core = place()
     seq_count, group_count = y_count * CORES, z_count * X
@@ -112,23 +109,18 @@
         pltpu.make_async_copy(grad.at[f], tokens.at[:, pl.ds(f * patches, patches)], load_sem.at[4]).start()
     pltpu.make_async_copy(weight, w, load_sem.at[5]).start()
 
-    lane, sub = iota((8, HALF), 1), iota((8, HALF), 0)
-    gs[...] = jnp.zeros_like(gs)
-
-    def put_gain(i):
-        at = lane == grp * share + i - core * HALF
-        gs[...] += jnp.where(at & (sub == 0), query_gain[i], 0.0) + jnp.where(at & (sub == 1), key_gain[i], 0.0)
-
-    loop(0, share, put_gain)
-    greet()
-
-    if z_count > 1:
-        loop(
-            1, z_count,
-            lambda d: remote(
-                gs, gz.at[z], gain_send.at[0], gain_recv.at[0], {"grp": x * z_count + lax.rem(z + d, z_count)}
-            ).start(),
+    small = [
+        pltpu.make_async_copy(ref, held_ref, load_sem.at[6 + i])
+        for i, (ref, held_ref) in enumerate(
+            ((query_gain_in, query_gain), (key_gain_in, key_gain), (clip_in, clip), (count_in, count))
         )
+    ]
+    for load in small:
+        load.start()
+    greeted = greet()
+
+    greeted()
+
     for load in loads:
         load.wait()
     for c in range(CHUNKS):
@@ -152,6 +144,24 @@
             win.at[c, 0, :, seq], recv_sem.at[c],
         ).start()
 
+    for load in small:
+        load.wait()
+
+    lane, sub = iota((8, HALF), 1), iota((8, HALF), 0)
+    gs[...] = jnp.zeros_like(gs)
+
+    def put_gain(i):
+        at = lane == grp * share + i - core * HALF
+        gs[...] += jnp.where(at & (sub == 0), query_gain[i], 0.0) + jnp.where(at & (sub == 1), key_gain[i], 0.0)
+
+    loop(0, share, put_gain)
+    if z_count > 1:
+        loop(
+            1, z_count,
+            lambda d: remote(
+                gs, gz.at[z], gain_send.at[0], gain_recv.at[0], {"grp": x * z_count + lax.rem(z + d, z_count)}
+            ).start(),
+        )
     def code_of(index, slot):
         at = (grp + (0, -1, 1)[slot]) * frames + index
         inside = (at >= 0) & (at < frames * group_count)
@@ -227,13 +237,15 @@
                         inverse = lax.rsqrt(mean_lanes(part * part) + EPS)
                         normed[a, h, slot] = (part * inverse * gain_of[h][a]).astype(bf16)
 
-                        @pl.when(slot == 0)
-                        def _():
+                        if isinstance(slot, int):
                             held[a, h] = part
                     else:
                         normed[a, h, slot] = part.astype(bf16)
 
-        loop(0, 3, gather)
+        gather(0)
+        for way in range(2):
+            halo(c, way).wait_recv()
+        loop(1, 3, gather)
         between[0]()
 
         def block(b, sums):
@@ -314,19 +326,23 @@
                 ring_copy(c, way, hop + 1).start()
             to_sibling(c, ref, ref)
 
-    def give_back(c):
+    def ring_start(c):
         for way in range(2):
             ring_copy(c, way, 0, att.at[c]).start()
         to_sibling(c, att.at[c], ag.at[c, core, y])
         pltpu.make_async_copy(att.at[c], ag.at[c, core, y], own_sem.at[c]).start()
+
+    def give_back(c, low, high):
         mine = rows_out.at[pl.ds(0, 3), y, :, pl.ds(pl.multiple_of(core * HALF + c * CH, HEAD_DIM), CH)]
 
-        def send(d):
-            other = lax.rem(seq + d, seq_count)
+        def send(i):
+            odd = lax.rem(i, 2)
+            other = lax.rem(seq + odd * lax.div(i + 1, 2) + (1 - odd) * (seq_count - lax.div(i, 2)), seq_count)
             remote(ret.at[c, :, other], mine, ret_send.at[c], ret_recv, {"seq": other}).start()
 
-        pltpu.make_async_copy(ret.at[c, :, seq], mine, ret_recv).start()
-        loop(1, seq_count, send)
+        if low == 0:
+            pltpu.make_async_copy(ret.at[c, :, seq], mine, ret_recv).start()
+        loop(max(low, 1), high, send)
 
     units = 2 * z_count
     turn[...] = jnp.zeros_like(turn)
@@ -345,15 +361,14 @@
             packed = hi_lo(terms[0:1] + terms[1:2], at_row, 0) + hi_lo(terms[2:3] + terms[3:4], at_row, 2)
             turn[pl.ds(width, POS)] = packed
             zall[kc, pl.ds(c * CH, CH)] = turn[...].T.astype(bf16)
-        if z_count > 1:
-            for unit in range(units * c // CHUNKS, units * (c + 1) // CHUNKS):
-                pair, owner = unit // z_count, unit % z_count
-
-                @pl.when(z != owner)
-                def _(unit=unit, pair=pair, owner=owner):
+        for unit in range(units * c // CHUNKS, units * (c + 1) // CHUNKS):
+            for kc in range(CORES):
+                owner = (2 * kc + unit // z_count) * z_count + unit % z_count
+
+                @pl.when(grp != owner)
+                def _(kc=kc, unit=unit, owner=owner):
                     remote(
-                        zall.at[:, pl.ds(unit * share, share)], zrecv.at[pair, z], z_send.at[pair], z_recv.at[pair],
-                        {"grp": x * z_count + owner},
+                        zall.at[kc, pl.ds(unit * share, share)], shares.at[grp], share_send, share_recv, {"grp": owner}
                     ).start()
 
     def project():
@@ -373,55 +388,48 @@
 
         loop(0, frames // 2, frame_pair)
 
-    def steps(*which):
-        def run():
-            for c, hop in which:
-                if hop < far:
-                    ring_step(c, hop)
-
-        return run
-
+    def part(eighths):
+        return seq_count * eighths // 8
+
+    def run(*events):
+        def go():
+            for event, c, *more in events:
+                if event == "step" and more[0] < far:
+                    ring_step(c, *more)
+                elif event == "ring":
+                    ring_start(c)
+                elif event == "ret":
+                    give_back(c, part(more[0]), part(more[1]))
+                elif event == "weigh":
+                    weigh(c)
+
+        return go
+
+    nothing = run()
     to_neighbours(0)
     wait_bytes(gx.at[pl.ds(0, X - 1)], gain_recv.at[1])
     gains[...] = jnp.sum(gx[...], axis=0)
     to_neighbours(1)
-    for way in range(2):
-        halo(0, way).wait_recv()
-    attend(0, (steps(), steps()))
-    give_back(0)
+    attend(0, (nothing, nothing))
+    run(("ring", 0), ("ret", 0, 0, 4))()
     to_neighbours(2)
-    for way in range(2):
-        halo(1, way).wait_recv()
-    attend(1, (steps((0, 0)), steps((0, 1))))
-    give_back(1)
-    for way in range(2):
-        halo(2, way).wait_recv()
-    attend(2, (steps((0, 2), (1, 0)), steps((0, 3), (1, 1))))
-    give_back(2)
+    attend(1, (run(("step", 0, 0), ("ret", 0, 4, 8)), nothing))
+    run(("ring", 1), ("step", 0, 1))()
+    attend(2, (run(("step", 0, 2), ("step", 1, 0)), nothing))
+    run(("ring", 2), ("step", 0, 3), ("step", 1, 1), ("step", 2, 0), ("ret", 1, 0, 4))()
     for load in (pltpu.make_async_copy(tokens, tokens, load_sem.at[4]), pltpu.make_async_copy(weight, w, load_sem.at[5])):
         load.wait()
-    steps((1, 2), (2, 0))()
-    weigh(0)
-    steps((1, 3), (2, 1))()
-    weigh(1)
-    steps((2, 2), (2, 3))()
-    weigh(2)
+    run(("weigh", 0), ("step", 1, 2), ("step", 2, 1), ("ret", 1, 4, 6), ("step", 1, 3), ("step", 2, 2), ("ret", 1, 6, 8), ("weigh", 1), ("step", 2, 3), ("weigh", 2), ("ret", 2, 0, 8))()
     project()
-    for pair in range(2):
-        if z_count > 1:
-            wait_bytes(zrecv.at[pair, pl.ds(0, z_count - 1)], z_recv.at[pair])
-        own = zall[:, pl.ds(pl.multiple_of((pair * z_count + z) * share, POS), share)]
-        zrecv[pair, z] = own
-        sums = jnp.sum(zrecv[pair].astype(f32), axis=0)
-        for kc in range(CORES):
-            xsend[2 * kc + pair] = sums[kc]
-
-    def last(d):
-        other = lax.rem(x + d, X)
-        remote(xsend.at[other], xrecv.at[x], x_send, x_recv, {"grp": other * z_count + z}).start()
-
-    loop(1, X, last)
-    xrecv[x] = xsend[x]
+    own_unit = lax.rem(x, 2) * z_count + z
+    shares[grp] = zall[lax.div(x, 2), pl.ds(pl.multiple_of(own_unit * share, POS), share)]
+    wait_bytes(shares.at[pl.ds(0, group_count - 1)], share_recv)
+    token_root = float(frames * patches * group_count) ** 0.5
+    total = jnp.sum(shares[...].astype(f32), axis=0) / token_root
+    wide_out[...] = total[:, :width]
+    terms = total.T
+    gain_out[0:1] = terms[width : width + 1] + terms[width + 1 : width + 2]
+    gain_out[1:2] = terms[width + 2 : width + 3] + terms[width + 3 : width + 4]
     for c in range(CHUNKS):
         wait_bytes(win.at[c, 0, :, pl.ds(0, seq_count - 1)], send_sem.at[c])
         wait_bytes(ret.at[c, :, pl.ds(0, seq_count - 1)], ret_send.at[c])
@@ -430,19 +438,22 @@
             halo(c, way).wait_send()
             for hop in range(far):
                 ring_copy(c, way, hop).wait_send()
-    if z_count > 1:
-        for pair in range(2):
-            wait_bytes(zrecv.at[pair, pl.ds(0, z_count - 1)], z_send.at[pair])
     wait_bytes(gx.at[pl.ds(0, X - 1)], gain_send.at[1])
+    wait_bytes(shares.at[pl.ds(0, group_count - 1)], share_send)
     wait_bytes(rows_out, ret_recv)
-    wait_bytes(xrecv.at[pl.ds(0, X - 1)], x_recv)
-    token_root = float(frames * patches * group_count) ** 0.5
-    total = jnp.sum(xrecv[...], axis=0) / token_root
-    wide_out[...] = total[:, :width]
-    terms = total.T
-    gain_out[0:1] = terms[width : width + 1] + terms[width + 1 : width + 2]
-    gain_out[1:2] = terms[width + 2 : width + 3] + terms[width + 3 : width + 4]
-    wait_bytes(xsend.at[pl.ds(0, X - 1)], x_send)
+
+
+def hand_out_kernel(rows_in, proj_in, wide_in, gain_in, *rest):
+    outs, sem = rest[:-1], rest[-1]
+    copies = [pltpu.make_async_copy(rows_in.at[i], outs[i], sem.at[i]) for i in range(4)]
+    copies.append(pltpu.make_async_copy(proj_in, outs[4], sem.at[4]))
+    for copy in copies:
+        copy.start()
+    outs[5][...] = wide_in[...]
+    for i in range(2):
+        outs[6 + i][...] = gain_in[i]
+    for copy in copies:
+        copy.wait()
 
 
 def body(
@@ -467,8 +478,7 @@
     rows = frames * POS
     wide = BLOCK_POS * frames
     far = y_count // 2
-    vmem, smem = pl.BlockSpec(memory_space=pltpu.VMEM), pl.BlockSpec(memory_space=pltpu.SMEM)
-    anywhere = pl.BlockSpec(memory_space=pl.ANY)
+    vmem, anywhere = pl.BlockSpec(memory_space=pltpu.VMEM), pl.BlockSpec(memory_space=pl.ANY)
     dma = pltpu.SemaphoreType.DMA
     rows_out, projected, wide_out, gain_out = pl.pallas_call(
         fused_kernel,
@@ -478,7 +488,7 @@
             jax.ShapeDtypeStruct((share, width), f32),
             jax.ShapeDtypeStruct((2, share), f32),
         ),
-        in_specs=[anywhere] * 4 + [smem] * 4 + [anywhere] * 2,
+        in_specs=[pl.BlockSpec(memory_space=pltpu.HBM)] * 10,
         out_specs=(anywhere, vmem, vmem, vmem),
         scratch_shapes=[
             pltpu.VMEM((4, y_count, POS, channels), bf16),
@@ -496,14 +506,16 @@
             pltpu.VMEM((width, channels), bf16),
             pltpu.VMEM((LANES, CH), f32),
             pltpu.VMEM((CORES, HALF, LANES), bf16),
-            pltpu.VMEM((2, z_count, CORES, share, LANES), bf16),
-            pltpu.VMEM((X, share, LANES), f32),
-            pltpu.VMEM((X, share, LANES), f32),
+            pltpu.VMEM((group_count, share, LANES), bf16),
             pltpu.VMEM((z_count, 8, HALF), f32),
             pltpu.VMEM((X, 8, HALF), f32),
             pltpu.VMEM((8, HALF), f32),
             pltpu.VMEM((8, HALF), f32),
-            dma((6,)),
+            pltpu.SMEM((share,), f32),
+            pltpu.SMEM((share,), f32),
+            pltpu.SMEM(clip_of_frame.shape, jnp.int32),
+            pltpu.SMEM(patch_count.shape, jnp.int32),
+            dma((10,)),
             dma((CHUNKS,)),
             dma((CHUNKS,)),
             dma((CHUNKS, 2)),
@@ -517,28 +529,38 @@
             dma((CHUNKS, 2, far)),
             dma((CHUNKS,)),
             dma((CHUNKS,)),
-            dma((2,)),
-            dma((2,)),
             dma,
             dma,
         ],
         compiler_params=pltpu.CompilerParams(collective_id=0, has_side_effects=True, vmem_limit_bytes=VMEM_LIMIT),
         name="fused",
     )(
-        *(a.reshape(y_count, POS, channels) for a in (query_rows, key_rows, value_rows, out_grad)),
-        query_gain, key_gain, clip_of_frame, patch_count, proj_grad, proj_weight,
+        *(
+            pltpu.with_memory_space_constraint(a, pltpu.HBM)
+            for a in (
+                *(a.reshape(y_count, POS, channels) for a in (query_rows, key_rows, value_rows, out_grad)),
+                query_gain, key_gain, clip_of_frame, patch_count, proj_grad, proj_weight,
+            )
+        )
     )
-    shape = (1, patches, channels)
-    return (
-        rows_out[3].reshape(shape),
-        projected,
-        rows_out[0].reshape(shape),
-        rows_out[1].reshape(shape),
-        rows_out[2].reshape(shape),
-        wide_out,
-        gain_out[0],
-        gain_out[1],
-    )
+    by_position = jax.ShapeDtypeStruct((y_count, POS, channels), bf16)
+    outs = pl.pallas_call(
+        hand_out_kernel,
+        out_shape=(by_position,) * 4
+        + (
+            jax.ShapeDtypeStruct(projected.shape, bf16),
+            jax.ShapeDtypeStruct(wide_out.shape, f32),
+            jax.ShapeDtypeStruct((share,), f32),
+            jax.ShapeDtypeStruct((share,), f32),
+        ),
+        in_specs=[vmem] * 4,
+        out_specs=(anywhere,) * 5 + (vmem,) * 3,
+        scratch_shapes=[dma((5,))],
+        compiler_params=pltpu.CompilerParams(vmem_limit_bytes=VMEM_LIMIT),
+        name="hand_out",
+    )(rows_out, projected, wide_out, gain_out)
+    query_grad, key_grad, value_grad, attended = (rows.reshape(1, patches, channels) for rows in outs[:4])
+    return attended, outs[4], query_grad, key_grad, value_grad, *outs[5:]
 
 
 def solution(mesh):

time: 137 us -> 123 us (0.90)
  Pallas kernels: 132 us -> 123 us
  local copies, waits for them, and re-layouts: 4.62 us -> 0 us
    pallas_call x1, Pallas kernels: 132 us -> 121 us  [body(): pl.pallas_call(fused_kernel, out_shape=(jax.ShapeDtypeStruct((4, y_count,...]
    slice x1 -> x0, local copies, waits for them, and re-layouts: 2.59 us -> none  [body(): rows_out[2].reshape(shape)]
    pallas_call x0 -> x1, Pallas kernels: none -> 2.07 us  [body(): pl.pallas_call(hand_out_kernel, out_shape=(by_position,) * 4 + (jax.Shape...]
    unnamed x8 -> x0, local copies, waits for them, and re-layouts: 1.51 us -> none
where the time goes in v3:
time: 123 us
  Pallas kernels  123 us (100%)
    pallas_call x1, Pallas kernels, body(): pl.pallas_call(fused_kernel, out_shape=(jax.ShapeDtypeStruct((4, y_count,...  121 us

profile of v3, /device:TPU:1, one launch (start us, length us, event | category | flops | bytes accessed | tf_op | source)
XLA Modules:
  0.0 123.3 jit_solution(7825132773554411680)
XLA Ops:
  0.6 120.6 %fused.1 = (bf16[4,8,16,1536]{3,2,1,0:T(8,128)(2,1)S(1)}, bf16[16,192,128]{2,1,0:T(8,128)(2,1)S(1)}, f32[48,192]{1,0:T(8,128)S(1)}, f32[2,48]{1,0:T(2,128)S(1)}) custom-call(bf16[8,16,1536]{2,1,0:T(8,128)(2,1)} %bitcast.8, bf16[8,16,1536]{2,1,0:T(8,128)(2,1)} %bitcast.9, bf16[8,16,1536]{2,1,0:T(8,128)(2,1)} %bitcast.10, bf16[8,16,1536]{2,1,0:T(8,128)(2,1)} %bitcast.11, ...), custom_call_target="tpu_custom_call" | custom-call | tf_op jit(solution)/shard_map/fused/pallas_call | solution.py:483
  121.3 2.1 %hand_out.1 = (bf16[8,16,1536]{2,1,0:T(8,128)(2,1)}, bf16[8,16,1536]{2,1,0:T(8,128)(2,1)}, bf16[8,16,1536]{2,1,0:T(8,128)(2,1)}, bf16[8,16,1536]{2,1,0:T(8,128)(...) custom-call(bf16[4,8,16,1536]{3,2,1,0:T(8,128)(2,1)S(1)} %get-tuple-element.20.rows_in, ...), custom_call_target="tpu_custom_call" | custom-call | tf_op jit(solution)/shard_map/hand_out/pallas_call | solution.py:547

commit v4 on v3

--- a/solution.py
+++ b/solution.py
@@ -102,13 +102,10 @@
     far = y_count // 2
     f32, bf16 = jnp.float32, jnp.bfloat16
 
+    greeted = greet()
     loads = [pltpu.make_async_copy(ref, stage.at[i], load_sem.at[i]) for i, ref in enumerate((q, k, v, g))]
     for load in loads:
         load.start()
-    for f in range(frames):
-        pltpu.make_async_copy(grad.at[f], tokens.at[:, pl.ds(f * patches, patches)], load_sem.at[4]).start()
-    pltpu.make_async_copy(weight, w, load_sem.at[5]).start()
-
     small = [
         pltpu.make_async_copy(ref, held_ref, load_sem.at[6 + i])
         for i, (ref, held_ref) in enumerate(
@@ -117,8 +114,6 @@
     ]
     for load in small:
         load.start()
-    greeted = greet()
-
     greeted()
 
     for load in loads:
@@ -144,6 +139,9 @@
             win.at[c, 0, :, seq], recv_sem.at[c],
         ).start()
 
+    for f in range(frames):
+        pltpu.make_async_copy(grad.at[f], tokens.at[:, pl.ds(f * patches, patches)], load_sem.at[4]).start()
+    pltpu.make_async_copy(weight, w, load_sem.at[5]).start()
     for load in small:
         load.wait()
 
@@ -411,15 +409,15 @@
     gains[...] = jnp.sum(gx[...], axis=0)
     to_neighbours(1)
     attend(0, (nothing, nothing))
-    run(("ring", 0), ("ret", 0, 0, 4))()
+    run(("ring", 0), ("ret", 0, 0, 8))()
     to_neighbours(2)
-    attend(1, (run(("step", 0, 0), ("ret", 0, 4, 8)), nothing))
+    attend(1, (run(("step", 0, 0)), nothing))
     run(("ring", 1), ("step", 0, 1))()
-    attend(2, (run(("step", 0, 2), ("step", 1, 0)), nothing))
-    run(("ring", 2), ("step", 0, 3), ("step", 1, 1), ("step", 2, 0), ("ret", 1, 0, 4))()
+    attend(2, (run(("step", 0, 2), ("step", 1, 0)), run(("ret", 1, 0, 3), ("step", 0, 3))))
+    run(("ring", 2), ("step", 1, 1), ("ret", 1, 3, 5), ("step", 2, 0))()
     for load in (pltpu.make_async_copy(tokens, tokens, load_sem.at[4]), pltpu.make_async_copy(weight, w, load_sem.at[5])):
         load.wait()
-    run(("weigh", 0), ("step", 1, 2), ("step", 2, 1), ("ret", 1, 4, 6), ("step", 1, 3), ("step", 2, 2), ("ret", 1, 6, 8), ("weigh", 1), ("step", 2, 3), ("weigh", 2), ("ret", 2, 0, 8))()
+    run(("weigh", 0), ("ret", 1, 5, 6), ("step", 1, 2), ("step", 2, 1), ("ret", 1, 6, 8), ("step", 1, 3), ("weigh", 1), ("step", 2, 2), ("ret", 2, 0, 4), ("step", 2, 3), ("weigh", 2), ("ret", 2, 4, 8))()
     project()
     own_unit = lax.rem(x, 2) * z_count + z
     shares[grp] = zall[lax.div(x, 2), pl.ds(pl.multiple_of(own_unit * share, POS), share)]

time: 123 us -> 120 us (0.976)
  Pallas kernels: 123 us -> 119 us
    pallas_call x1, Pallas kernels: 121 us -> 117 us  [body(): pl.pallas_call(fused_kernel, out_shape=(jax.ShapeDtypeStruct((4, y_count,...]
where the time goes in v4:
time: 120 us; the launch traced here: 119 us
  Pallas kernels  119 us (99%)
    pallas_call x1, Pallas kernels, body(): pl.pallas_call(fused_kernel, out_shape=(jax.ShapeDtypeStruct((4, y_count,...  117 us

profile of v4, /device:TPU:1, one launch (start us, length us, event | category | flops | bytes accessed | tf_op | source)
XLA Modules:
  0.0 119.4 jit_solution(15741659638112987258)
XLA Ops:
  0.6 116.7 %fused.1 = (bf16[4,8,16,1536]{3,2,1,0:T(8,128)(2,1)S(1)}, bf16[16,192,128]{2,1,0:T(8,128)(2,1)S(1)}, f32[48,192]{1,0:T(8,128)S(1)}, f32[2,48]{1,0:T(2,128)S(1)}) custom-call(bf16[8,16,1536]{2,1,0:T(8,128)(2,1)} %bitcast.8, bf16[8,16,1536]{2,1,0:T(8,128)(2,1)} %bitcast.9, bf16[8,16,1536]{2,1,0:T(8,128)(2,1)} %bitcast.10, bf16[8,16,1536]{2,1,0:T(8,128)(2,1)} %bitcast.11, ...), custom_call_target="tpu_custom_call" | custom-call | tf_op jit(solution)/shard_map/fused/pallas_call | solution.py:481
  117.3 2.1 %hand_out.1 = (bf16[8,16,1536]{2,1,0:T(8,128)(2,1)}, bf16[8,16,1536]{2,1,0:T(8,128)(2,1)}, bf16[8,16,1536]{2,1,0:T(8,128)(2,1)}, bf16[8,16,1536]{2,1,0:T(8,128)(...) custom-call(bf16[4,8,16,1536]{3,2,1,0:T(8,128)(2,1)S(1)} %get-tuple-element.20.rows_in, ...), custom_call_target="tpu_custom_call" | custom-call | tf_op jit(solution)/shard_map/hand_out/pallas_call | solution.py:545

commit v5 on v4

--- a/solution.py
+++ b/solution.py
@@ -129,7 +129,7 @@
                     send_sem.at[c], recv_sem.at[c], {"seq": other * CORES + cc},
                 ).start()
 
-        loop(1, y_count, spread_out)
+        loop(1, y_count, lambda i, spread_out=spread_out: spread_out(y_count - i))
         remote(
             stage.at[:, y, :, pl.ds(pl.multiple_of((1 - core) * HALF + c * CH, HEAD_DIM), CH)],
             win.at[c, 0, :, seq], send_sem.at[c], recv_sem.at[c], {"seq": y * CORES + 1 - core},
@@ -389,6 +389,15 @@
     def part(eighths):
         return seq_count * eighths // 8
 
+    def drain(c):
+        wait_bytes(win.at[c, 0, :, pl.ds(0, seq_count - 1)], send_sem.at[c])
+        for way in range(2):
+            halo(c, way).wait_send()
+            for hop in range(far):
+                ring_copy(c, way, hop).wait_send()
+        wait_bytes(ag.at[c, core], sib_send.at[c])
+        wait_bytes(ret.at[c, :, pl.ds(0, seq_count - 1)], ret_send.at[c])
+
     def run(*events):
         def go():
             for event, c, *more in events:
@@ -419,6 +428,9 @@
         load.wait()
     run(("weigh", 0), ("ret", 1, 5, 6), ("step", 1, 2), ("step", 2, 1), ("ret", 1, 6, 8), ("step", 1, 3), ("weigh", 1), ("step", 2, 2), ("ret", 2, 0, 4), ("step", 2, 3), ("weigh", 2), ("ret", 2, 4, 8))()
     project()
+    for c in range(CHUNKS - 1):
+        drain(c)
+    wait_bytes(gx.at[pl.ds(0, X - 1)], gain_send.at[1])
     own_unit = lax.rem(x, 2) * z_count + z
     shares[grp] = zall[lax.div(x, 2), pl.ds(pl.multiple_of(own_unit * share, POS), share)]
     wait_bytes(shares.at[pl.ds(0, group_count - 1)], share_recv)
@@ -428,23 +440,20 @@
     terms = total.T
     gain_out[0:1] = terms[width : width + 1] + terms[width + 1 : width + 2]
     gain_out[1:2] = terms[width + 2 : width + 3] + terms[width + 3 : width + 4]
-    for c in range(CHUNKS):
-        wait_bytes(win.at[c, 0, :, pl.ds(0, seq_count - 1)], send_sem.at[c])
-        wait_bytes(ret.at[c, :, pl.ds(0, seq_count - 1)], ret_send.at[c])
-        wait_bytes(ag.at[c, core], sib_send.at[c])
-        for way in range(2):
-            halo(c, way).wait_send()
-            for hop in range(far):
-                ring_copy(c, way, hop).wait_send()
-    wait_bytes(gx.at[pl.ds(0, X - 1)], gain_send.at[1])
+    drain(CHUNKS - 1)
     wait_bytes(shares.at[pl.ds(0, group_count - 1)], share_send)
     wait_bytes(rows_out, ret_recv)
 
 
 def hand_out_kernel(rows_in, proj_in, wide_in, gain_in, *rest):
     outs, sem = rest[:-1], rest[-1]
-    copies = [pltpu.make_async_copy(rows_in.at[i], outs[i], sem.at[i]) for i in range(4)]
-    copies.append(pltpu.make_async_copy(proj_in, outs[4], sem.at[4]))
+    parts = [(rows_in.at[i], outs[i]) for i in range(4)] + [(proj_in, outs[4])]
+    copies = []
+    for src, dst in parts:
+        half = src.shape[0] // 2
+        for low in (0, half):
+            at = pl.ds(low, half)
+            copies.append(pltpu.make_async_copy(src.at[at], dst.at[at], sem.at[len(copies)]))
     for copy in copies:
         copy.start()
     outs[5][...] = wide_in[...]
@@ -553,7 +562,7 @@
         ),
         in_specs=[vmem] * 4,
         out_specs=(anywhere,) * 5 + (vmem,) * 3,
-        scratch_shapes=[dma((5,))],
+        scratch_shapes=[dma((10,))],
         compiler_params=pltpu.CompilerParams(vmem_limit_bytes=VMEM_LIMIT),
         name="hand_out",
     )(rows_out, projected, wide_out, gain_out)

time: 120 us -> 118 us (0.983)
  Pallas kernels: 119 us -> 117 us
    pallas_call x1, Pallas kernels: 117 us -> 115 us  [body(): pl.pallas_call(fused_kernel, out_shape=(jax.ShapeDtypeStruct((4, y_count,...]
where the time goes in v5:
time: 118 us
  Pallas kernels  117 us (99%)
    pallas_call x1, Pallas kernels, body(): pl.pallas_call(fused_kernel, out_shape=(jax.ShapeDtypeStruct((4, y_count,...  115 us

profile of v5, /device:TPU:1, one launch (start us, length us, event | category | flops | bytes accessed | tf_op | source)
XLA Modules:
  0.0 118.0 jit_solution(2277133638321747362)
XLA Ops:
  0.6 115.2 %fused.1 = (bf16[4,8,16,1536]{3,2,1,0:T(8,128)(2,1)S(1)}, bf16[16,192,128]{2,1,0:T(8,128)(2,1)S(1)}, f32[48,192]{1,0:T(8,128)S(1)}, f32[2,48]{1,0:T(2,128)S(1)}) custom-call(bf16[8,16,1536]{2,1,0:T(8,128)(2,1)} %bitcast.8, bf16[8,16,1536]{2,1,0:T(8,128)(2,1)} %bitcast.9, bf16[8,16,1536]{2,1,0:T(8,128)(2,1)} %bitcast.10, bf16[8,16,1536]{2,1,0:T(8,128)(2,1)} %bitcast.11, ...), custom_call_target="tpu_custom_call" | custom-call | tf_op jit(solution)/shard_map/fused/pallas_call | solution.py:490
  115.9 2.1 %hand_out.1 = (bf16[8,16,1536]{2,1,0:T(8,128)(2,1)}, bf16[8,16,1536]{2,1,0:T(8,128)(2,1)}, bf16[8,16,1536]{2,1,0:T(8,128)(2,1)}, bf16[8,16,1536]{2,1,0:T(8,128)(...) custom-call(bf16[4,8,16,1536]{3,2,1,0:T(8,128)(2,1)S(1)} %get-tuple-element.20.rows_in, ...), custom_call_target="tpu_custom_call" | custom-call | tf_op jit(solution)/shard_map/hand_out/pallas_call | solution.py:554
